TPU v7x, 32 devices: a whole 2x2x4 slice. The times are simulated.
32 devices in a mesh: dp: 4 (over x, core), expert: 8 (over z, y).
Axes of the slice: x: 2, y: 2, z: 4, core: 2. Of those that a mesh axis runs over, the one named last changes fastest.
Arguments:
- tokens: bfloat16 [4, 1024, 4096], P('dp', 'expert'), may hold values from -6 to 6
- norm_gain: float32 [4096], replicated, may hold values from 0.5 to 1.5
- router_weight: float32 [8, 4096], replicated, may hold values from -0.09375 to 0.09375
- value_weight: float32 [4096], replicated, may hold values from -0.09375 to 0.09375
- gate_weight: bfloat16 [8, 1536, 4096], P('expert', 'dp'), may hold values from -0.09375 to 0.09375
- up_weight: bfloat16 [8, 1536, 4096], P('expert', 'dp'), may hold values from -0.09375 to 0.09375
- down_weight: bfloat16 [8, 1536, 4096], P('expert', 'dp'), may hold values from -0.15625 to 0.15625
- routes: int32 [4, 1024, 2], P('dp', 'expert'), may hold values from 0 to 7, all different within a row; in each aligned block of 128 rows (0 to 127, 128 to 255, ..., all dimensions but the last counted through in order) at most 48 rows name the same one
- segment_ids: int32 [4, 1024], P('dp', 'expert'), may hold values from 0 to 7, never falling along the last dimension, each value on 1 to 256 neighbouring positions
- loss_mask: int32 [4, 1024], P('dp', 'expert'), may hold values 0 or 1
- penalty_reward: float32 [4, 1024], P('dp', 'expert'), may hold values from -0.3 to 0.3
- scores: float32 [4, 8], P('dp'), may hold values from -6 to 6
Outputs:
- values: float32 [4, 1024], P('dp', 'expert')
- mean_loss: float32 [], replicated
- value_grad: float32 [4096], replicated
- router_grad: float32 [8, 4096], replicated
- gate_grad: bfloat16 [8, 1536, 4096], P('expert', 'dp')
- up_grad: bfloat16 [8, 1536, 4096], P('expert', 'dp')
- down_grad: bfloat16 [8, 1536, 4096], P('expert', 'dp')
Inputs may be any that keep to these rules, and one draw needn't show every extreme that they name: Each token names 2 different experts; within the tokens of one device no expert is named by more than 48 routes, a bound that some block reaches. `segment_ids`: within each data row the ids never fall; each response holds 1 to 256 tokens and one holds exactly 256.
All inputs are finite; a program needn't handle non-finite values. No bound on the sum of `loss_mask` on one device may be relied on, other than what follows from the above.
Results may differ from a plain program's by a relative error of at most 0.0069.
Values may be sent and summed in bfloat16 or wider, within the bound.
A program may use at most 192 MiB of HBM per device.

v0:
```python
import jax
import jax.numpy as jnp
from jax import lax
from jax.sharding import PartitionSpec as P

discount_rate = 0.9995
norm_epsilon = 1e-06
white_epsilon = 1e-05
highest = lax.Precision.HIGHEST


def passed_along(array, axis, by):
    size = lax.axis_size(axis)
    pairs = [(i, i + by) for i in range(size) if 0 <= i + by < size]
    return lax.ppermute(array, axis, pairs)


def entering(part, axis, combine, identity):
    count = lax.axis_size(axis)
    place = lax.axis_index(axis)
    ahead = count - 1 - place
    gathered = jax.tree.map(lambda a: lax.all_gather(a, axis), part)
    state = jax.tree.map(lambda a, e: jnp.zeros_like(a) + jnp.asarray(e, a.dtype), part, identity)

    def one(turn, state):
        source = count - 1 - turn
        return combine(
            state, jax.tree.map(lambda a: lax.dynamic_index_in_dim(a, source, 0, False), gathered)
        )

    return lax.fori_loop(0, ahead, one, state)


def norm_rows(tokens, norm_gain):
    as_float = tokens.astype(jnp.float32)
    inverse_rms = lax.rsqrt(jnp.mean(as_float * as_float, axis=-1, keepdims=True) + norm_epsilon)
    return (as_float * inverse_rms * norm_gain).astype(jnp.bfloat16)


def slot_numbers(block_routes, experts):
    flattened = block_routes.reshape(-1)
    onehot = (flattened[:, None] == jnp.arange(experts, dtype=jnp.int32)[None, :]).astype(jnp.int32)
    before = jnp.cumsum(onehot, axis=0) - onehot
    return jnp.sum(before * onehot, axis=1).reshape(block_routes.shape)


def compose(earlier, later):
    return (later[0] * earlier[0], later[1] + later[0] * earlier[1])


def shards(
    tokens,
    norm_gain,
    router_weight,
    value_weight,
    gate_weight,
    up_weight,
    down_weight,
    routes,
    segment_ids,
    loss_mask,
    penalty_reward,
    scores,
):
    tok_count = tokens.shape[1]
    model_width = tokens.shape[2]
    route_count = routes.shape[2]
    experts = router_weight.shape[0]
    hidden_width = gate_weight.shape[1]
    dp_count = lax.axis_size("dp")
    expert_count = lax.axis_size("expert")
    capacity = tok_count * route_count * 3 // (2 * experts)
    last_last = (((1,), (1,)), ((), ()))
    first_first = (((0,), (0,)), ((), ()))
    own_tokens = tokens[0]
    own_routes = routes[0]
    normed = norm_rows(own_tokens, norm_gain)
    logits = lax.dot_general(
        normed.astype(jnp.float32), router_weight, last_last, precision=highest
    )
    chosen = jnp.take_along_axis(logits, own_routes, axis=1)
    gate_sigmoid = jax.nn.sigmoid(chosen)
    sigmoid_total = jnp.sum(gate_sigmoid, axis=1, keepdims=True)
    route_prob = gate_sigmoid / sigmoid_total
    slot_number = slot_numbers(own_routes, experts)
    slot_place = (own_routes * capacity + slot_number).reshape(-1)
    token_ids = jnp.broadcast_to(jnp.arange(tok_count, dtype=jnp.int32)[:, None], own_routes.shape)
    source_index = (
        jnp.full((experts * capacity,), tok_count, jnp.int32)
        .at[slot_place]
        .set(token_ids.reshape(-1))
    )
    outgoing = jnp.take(normed, source_index, axis=0, mode="fill", fill_value=0).reshape(
        experts, capacity, model_width
    )
    incoming = lax.all_to_all(outgoing, "expert", split_axis=0, concat_axis=0, tiled=True)
    expert_rows = lax.all_gather(incoming[None], "dp", axis=0, tiled=True).reshape(-1, model_width)
    both_weights = jnp.concatenate([gate_weight[0], up_weight[0]], axis=0)
    both_values = lax.dot_general(
        expert_rows, both_weights, last_last, preferred_element_type=jnp.float32
    )
    gate_value = both_values[:, :hidden_width]
    up_value = both_values[:, hidden_width:]
    gate_sig = jax.nn.sigmoid(gate_value)
    hidden = (gate_value * gate_sig * up_value).astype(jnp.bfloat16)
    down_float = down_weight[0].astype(jnp.float32)
    value_along = jnp.dot(down_float, value_weight, precision=highest)
    partial_value = jnp.dot(hidden.astype(jnp.float32), value_along, precision=highest)
    partial_value = partial_value.reshape(dp_count, expert_count, capacity)
    summed = lax.psum_scatter(partial_value, "dp", scatter_dimension=0, tiled=True)
    returned = lax.all_to_all(summed, "expert", split_axis=1, concat_axis=1, tiled=True)[0]
    route_value = returned.reshape(-1)[slot_place].reshape(tok_count, route_count)
    own_values = jnp.dot(own_tokens.astype(jnp.float32), value_weight, precision=highest) + jnp.sum(
        route_prob * route_value, axis=1
    )
    segment = segment_ids[0]
    marker = passed_along(segment[:1] + 1, "expert", -1)
    carries = marker[0] == segment[-1] + 1
    following = jnp.concatenate([segment[1:], jnp.where(carries, segment[-1:], -1)])
    ending = following != segment
    segment_hit = segment[:, None] == jnp.arange(scores.shape[1], dtype=jnp.int32)[None, :]
    score_pick = jnp.sum(jnp.where(segment_hit, scores[0][None, :], 0.0), axis=1)
    reward = penalty_reward[0] + jnp.where(ending, score_pick, 0.0)
    position = jnp.arange(tok_count, dtype=jnp.int32)
    offset = (position[None, :] - position[:, None]).astype(jnp.float32)
    log_rate = jnp.log(jnp.float32(discount_rate))
    same_segment = (segment[:, None] == segment[None, :]) & (offset >= 0.0)
    discount = jnp.where(same_segment, jnp.exp(offset * log_rate), 0.0)
    local_return = jnp.dot(discount, reward, precision=highest)
    reach = jnp.where(
        (segment == segment[-1]) & carries,
        jnp.exp((tok_count - position).astype(jnp.float32) * log_rate),
        0.0,
    )
    identity = (jnp.ones((), jnp.float32), jnp.zeros((), jnp.float32))
    carry_in = entering((reach[0], local_return[0]), "expert", compose, identity)[1]
    returns = local_return + reach * carry_in
    mask_float = loss_mask[0].astype(jnp.float32)
    token_total, return_total = lax.psum(
        (jnp.sum(mask_float), jnp.sum(mask_float * returns)), ("dp", "expert")
    )
    divisor = jnp.maximum(token_total, 1.0)
    centre = return_total / divisor
    deviation = returns - centre
    spread_total = lax.psum(jnp.sum(mask_float * deviation * deviation), ("dp", "expert"))
    variance = spread_total / divisor
    whitened = (returns - centre) * lax.rsqrt(variance + white_epsilon)
    value_error = mask_float * (own_values - whitened)
    loss_part = 0.5 * jnp.sum(mask_float * (own_values - whitened) * (own_values - whitened))
    route_weight = value_error[:, None] * route_prob
    prob_grad = value_error[:, None] * route_value
    weight_table = (
        jnp.zeros((experts * capacity,), jnp.float32)
        .at[slot_place]
        .set(route_weight.reshape(-1))
        .reshape(experts, capacity)
    )
    owner_weight = lax.all_to_all(weight_table, "expert", split_axis=0, concat_axis=0, tiled=True)
    owner_weight = lax.all_gather(owner_weight[None], "dp", axis=0, tiled=True)
    row_weight = owner_weight.reshape(-1)
    spread = jnp.dot(row_weight, hidden.astype(jnp.float32), precision=highest)
    down_grad = (spread[:, None] * value_weight[None, :]).astype(jnp.bfloat16)
    hidden_grad = row_weight[:, None] * value_along[None, :]
    gate_delta = (hidden_grad * up_value * gate_sig * (1.0 + gate_value * (1.0 - gate_sig))).astype(
        jnp.bfloat16
    )
    up_delta = (hidden_grad * gate_value * gate_sig).astype(jnp.bfloat16)
    both_delta = jnp.concatenate([gate_delta, up_delta], axis=1)
    both_grad = lax.dot_general(
        both_delta, expert_rows, first_first, preferred_element_type=jnp.float32
    ).astype(jnp.bfloat16)
    gate_grad = both_grad[:hidden_width]
    up_grad = both_grad[hidden_width:]
    sigma_grad = (
        prob_grad - jnp.sum(prob_grad * route_prob, axis=1, keepdims=True)
    ) / sigmoid_total
    chosen_grad = sigma_grad * gate_sigmoid * (1.0 - gate_sigmoid)
    expert_hit = own_routes[:, :, None] == jnp.arange(experts, dtype=jnp.int32)[None, None, :]
    logit_grad = jnp.sum(jnp.where(expert_hit, chosen_grad[:, :, None], 0.0), axis=1)
    router_part = lax.dot_general(
        logit_grad, normed.astype(jnp.float32), first_first, precision=highest
    )
    value_part = jnp.dot(value_error, own_tokens.astype(jnp.float32), precision=highest) + jnp.dot(
        spread, down_float, precision=highest
    )
    router_grad, value_grad, loss_total = lax.psum(
        (router_part, value_part, loss_part), ("dp", "expert")
    )
    mean_loss = loss_total / divisor
    return (
        own_values[None],
        mean_loss,
        value_grad,
        router_grad,
        gate_grad[None],
        up_grad[None],
        down_grad[None],
    )


def solution(mesh):
    placed = (
        P("dp", "expert", None),
        P(),
        P(),
        P(),
        P("expert", "dp", None),
        P("expert", "dp", None),
        P("expert", "dp", None),
        P("dp", "expert", None),
        P("dp", "expert"),
        P("dp", "expert"),
        P("dp", "expert"),
        P("dp", None),
    )
    return jax.shard_map(
        shards,
        mesh=mesh,
        in_specs=placed,
        out_specs=(
            P("dp", "expert"),
            P(),
            P(),
            P(),
            P("expert", "dp", None),
            P("expert", "dp", None),
            P("expert", "dp", None),
        ),
        check_vma=False,
    )
```

profile of v0, /device:TPU:0, one launch (start us, length us, event | category | flops | bytes accessed | tf_op | source)
XLA Modules:
  0.0 433.4 jit_solution(5520542179357791941)
XLA Ops:
  7.2 0.8 broadcast_multiply_fusion
  8.1 0.9 copy.43
  10.6 1.4 scatter_custom_fusion
  12.0 1.5 fusion.16
  13.6 2.5 fusion.18
  16.2 9.6 %gather_fusion = bf16[384,4096]{1,0:T(8,128)(2,1)} fusion(bf16[128,4096]{1,0:T(8,128)(2,1)} %fusion.18, s32[1024]{0:T(1024)S(1)} %pad_clamp_fusion.1), kind=kCustom, calls=%fused_computation | custom fusion | bytes 6292992 | tf_op jit(solution)/shard_map/jit(_take)/gather | solution.py:93
  25.8 2.2 broadcast_select_fusion
  27.9 77.9 %all_to_all.19 = bf16[8,48,4096]{2,1,0:T(8,128)(2,1)} all-to-all(bf16[8,48,4096]{2,1,0:T(8,128)(2,1)S(1)} %broadcast_select_fusion), channel_id=1, replica_groups=mesh['dp'=4,'expert'=8] {'expert'}, dimensions={0} | all-to-all | bytes 6291456 | tf_op jit(solution)/shard_map/all_to_all | solution.py:96
  107.7 1.3 collective-permute-start
  109.3 2.1 fusion.64
  111.5 1.4 gather_fusion.2
  115.2 2.6 fusion.62
  119.3 0.8 slice_dynamic-update-slice_fusion.1
  120.1 0.7 and_select_fusion.1
  120.8 0.7 slice_dynamic-update-slice_fusion
  122.1 21.6 %all-reduce.5 = (f32[8]{0:T(128)S(1)}, f32[8]{0:T(128)S(1)}) all-reduce(f32[8]{0:T(128)S(1)} %slice_dynamic-update-slice_fusion.1, f32[8]{0:T(128)S(1)} %slice_dynamic-update-slice_fusion), channel_id=1, replica_groups=mesh['dp'=4,'expert'=8] {'expert'}, use_global_device_ids=true, to_apply=%add | all-reduce | flops 16 | bytes 128
  143.7 17.1 %while.14 = (s32[]{:T(128)}, f32[]{:T(128)}, s32[]{:T(128)}, f32[8]{0:T(128)S(1)}, f32[8]{0:T(128)S(1)}, /*index=5*/s32[]{:T(128)}, s32[]{:T(128)}, s32[]{:T(128)}, s32[]{:T(128)}) while((s32[]{:T(128)}, f32[]{:T(128)}, s32[]{:T(128)}, f32[8]{0:T(128)S(1)}, f32[8]{0:T(128)S(1)}, /*index=5*/s32[]{:T(128)}, s32[]{:T(128)}, s32[]{:T(128)}, ...), condition=%wide.region_10.11_spmd, body=%wide.region_9.10_spmd.sunk | while | flops 8 | bytes 195 | solution.py:31
  151.0 0.7 dynamic_slice.17
  160.8 1.3 fusion.53
  162.0 37.5 %all-reduce.4 = (f32[]{:T(128)}, f32[]{:T(128)}) all-reduce(f32[]{:T(128)} %get-tuple-element.110, f32[]{:T(128)} %convert_reduce_fusion), channel_id=1, replica_groups=mesh['dp'=4,'expert'=8] {'dp','expert'}, use_global_device_ids=true, to_apply=%region_12.13 | all-reduce | flops 2 | bytes 16 | tf_op jit(solution)/shard_map/psum | solution.py:139
  200.8 13.9 %fusion = f32[1536,768]{0,1:T(8,128)S(1)} fusion(bf16[1536,4096]{1,0:T(8,128)(2,1)} %bitcast.126, bf16[384,4096]{1,0:T(8,128)(2,1)} %bitcast.128, bf16[384,4096]{1,0:T(8,128)(2,1)} %bitcast.129), kind=kOutput, calls=%fused_computation.6 | convolution fusion | flops 9676259328 | bytes 23592960 | tf_op jit(solution)/shard_map/dot_general | solution.py:99
  214.8 2.1 copy-done.1
  216.8 0.7 multiply_convert_fusion.1
  217.6 1.0 copy-done.2
  219.3 11.1 %all-reduce.2 = f32[4,8,48]{2,1,0:T(8,128)S(1)} all-reduce(f32[4,8,48]{2,1,0:T(8,128)S(1)} %reshape.275), channel_id=4, replica_groups=mesh['dp'=4,'expert'=8] {'dp'}, use_global_device_ids=true, to_apply=%region_6.7.clone | all-reduce | flops 1536 | bytes 12288
  230.4 1.2 constant_dynamic-slice_fusion
  231.6 5.1 %all-to-all-start.1 = ((f32[1,8,48]{2,0,1:T(1,128)}), f32[1,8,48]{2,0,1:T(1,128)S(1)}, u32[]{:S(2)}, u32[]{:S(2)}) async-start(f32[1,8,48]{2,0,1:T(1,128)} %bitcast.17), calls=%async_computation.1 | async-start | bytes 8192 | tf_op jit(solution)/shard_map/all_to_all | solution.py:111
  237.6 41.2 %psum.44 = f32[]{:T(128)} all-reduce(f32[]{:T(128)} %fusion.48), channel_id=1, replica_groups=mesh['dp'=4,'expert'=8] {'dp','expert'}, use_global_device_ids=true, to_apply=%region_16.17 | all-reduce | flops 1 | bytes 8 | tf_op jit(solution)/shard_map/psum | solution.py:145
  279.9 0.7 reduce.15
  280.7 1.9 gather_fusion.1
  282.9 3.3 multiply_reduce_fusion.2
  286.4 1.4 scatter_custom_fusion.1
  287.8 0.7 all_to_all.14
  288.5 5.5 %all-to-all-start.2 = ((f32[8,1,48]{2,1,0:T(1,128)}), f32[8,1,48]{2,1,0:T(1,128)S(1)}, u32[]{:S(2)}, u32[]{:S(2)}) async-start(f32[8,1,48]{2,1,0:T(1,128)} %all_to_all.14), calls=%async_computation.2 | async-start | bytes 8192 | tf_op jit(solution)/shard_map/all_to_all | solution.py:158
  294.1 2.4 fusion.65
  296.5 1.7 fusion.20
  298.9 1.5 all-to-all-done.2
  300.4 5.4 %all-gather.1 = f32[32,1,48]{2,1,0:T(1,128)S(1)} all-gather(f32[8,1,48]{2,1,0:T(1,128)S(1)} %all-to-all-done.2), channel_id=3, replica_groups=mesh['dp'=4,'expert'=8] {'dp'}, dimensions={0}, use_global_device_ids=true | all-gather | bytes 7680 | tf_op jit(solution)/shard_map/all_gather | solution.py:159
  305.8 0.7 reduce.16
  306.6 2.3 fusion.63
  308.9 1.3 fusion.4
  310.3 3.5 fusion.10
  313.8 13.1 %convolution_convert_fusion = bf16[768,4096]{1,0:T(8,128)(2,1)S(1)} fusion(bf16[1536,4096]{1,0:T(8,128)(2,1)} %bitcast.127, bf16[1536,384]{0,1:T(8,128)(2,1)S(1)} %get-tuple-element.119, bf16[1536,384]{0,1:T(8,128)(2,1)S(1)} %get-tuple-element.118), kind=kOutput, calls=%fused_computation.5 | convolution fusion | flops 9671540736 | bytes 21233664 | tf_op jit(solution)/shard_map/dot_general | solution.py:169
  326.9 3.5 slice_bitcast_fusion
  330.4 2.3 multiply_convert_fusion
  332.7 38.6 %all-reduce.3 = (f32[]{:T(128)}, f32[4096]{0:T(1024)}) all-reduce(f32[]{:T(128)S(6)} %mul_shard_map.3, f32[4096]{0:T(1024)S(1)} %add.167), channel_id=1, replica_groups=mesh['dp'=4,'expert'=8] {'dp','expert'}, use_global_device_ids=true, to_apply=%region_18.19 | all-reduce | flops 4097 | bytes 32776 | tf_op jit(solution)/shard_map/psum | solution.py:186
  372.0 52.0 %all-reduce.8.cloned.1.call-done = f32[8,4096]{1,0:T(8,128)} async-done(((f32[8,4096]{1,0:T(8,128)}), f32[8,4096]{1,0:T(8,128)}) %all-reduce.8.cloned.1.call-update) | async-done | bytes 131088 | tf_op jit(solution)/shard_map/psum | solution.py:186
  423.9 1.6 copy.63
  (95 shorter events, 16.4 us)
Async XLA Ops:
  7.2 108.0 %copy-start = (bf16[1,384,4096]{2,1,0:T(8,128)(2,1)S(1)}, bf16[1,384,4096]{2,1,0:T(8,128)(2,1)}, u32[]{:S(2)}) copy-start(bf16[1,384,4096]{2,1,0:T(8,128)(2,1)} %param.20) | copy-start | bytes 9437188
  7.2 193.6 %all-gather.4.cloned.1.call-start = ((), (), s32[]{:S(2)}) async-start(), calls=%async_computation.4 | async-start | bytes 15728640 | tf_op jit(solution)/shard_map/all_gather | solution.py:97
  105.8 0.7 copy-start.6
  105.8 3.2 copy-start.5
  105.8 3.5 copy-start.4
  107.7 10.1 %collective-permute-start = (s32[1]{0:T(128)}, s32[1]{0:T(128)}, u32[]{:S(2)}, u32[]{:S(2)}) collective-permute-start(s32[1]{0:T(128)} %bitcast.23), channel_id=1, source_target_pairs={{1,0},{2,1},{3,2},{4,3},{5,4},{6,5},{7,6},{9,8},{10,9},{11,10},{12... | collective-permute-start | bytes 20 | tf_op jit(solution)/shard_map/ppermute | solution.py:15
  111.4 2.3 copy-start.11
  111.4 2.9 copy-start.7
  111.5 3.6 copy-start.8
  111.5 3.7 copy-start.3
  112.9 6.2 %copy-start.9 = (f32[1,128]{1,0:T(1,128)S(1)}, f32[1,128]{1,0:T(1,128)}, u32[]{:S(2)}) copy-start(f32[1,128]{1,0:T(1,128)} %param.24) | copy-start | bytes 1540
  112.9 8.7 %copy-start.10 = (u32[32]{0:T(128)S(1)}, u32[32]{0:T(128)}, u32[]{:S(2)}) copy-start(u32[32]{0:T(128)} %constant.142) | copy-start | bytes 388
  214.7 2.1 copy-start.1
  217.6 1.0 copy-start.2
  231.6 47.8 %all-to-all-start.1 = ((f32[1,8,48]{2,0,1:T(1,128)}), f32[1,8,48]{2,0,1:T(1,128)S(1)}, u32[]{:S(2)}, u32[]{:S(2)}) async-start(f32[1,8,48]{2,0,1:T(1,128)} %bitcast.17), calls=%async_computation.1 | async-start | bytes 8192 | tf_op jit(solution)/shard_map/all_to_all | solution.py:111
  288.5 11.9 %all-to-all-start.2 = ((f32[8,1,48]{2,1,0:T(1,128)}), f32[8,1,48]{2,1,0:T(1,128)S(1)}, u32[]{:S(2)}, u32[]{:S(2)}) async-start(f32[8,1,48]{2,1,0:T(1,128)} %all_to_all.14), calls=%async_computation.2 | async-start | bytes 8192 | tf_op jit(solution)/shard_map/all_to_all | solution.py:158
  294.0 129.9 %all-reduce.8.cloned.1.call-start = ((), (), s32[]{:S(2)}) async-start(), calls=%async_computation.3 | async-start | bytes 262144 | tf_op jit(solution)/shard_map/psum | solution.py:186
Sparse Core Ops, SparseCore 0:
  106.0 81.7 all-gather.3
  301.0 122.9 all-reduce.7
where the time goes:
time: 435 us; the launch traced here: 433 us
  blocking collectives  233 us (54%)
  waiting for transfers between devices  53.5 us (12%)
  matrix products  43.6 us (10%)
  local copies, waits for them, and re-layouts  42 us (10%)
  between operations  21.5 us (5%)
  other arithmetic  19.1 us (4%)
  starting transfers between devices  12 us (3%)
  loops' own time  8.6 us (2%)
    all_to_all x1, blocking collectives, shards(): lax.all_to_all(outgoing, 'expert', split_axis=0, concat_axis=0, tiled=True)  77.9 us
    psum x1, waiting for transfers between devices, shards(): lax.psum((router_part, value_part, loss_part), ('dp', 'expert'))  52 us
    psum x1, blocking collectives, shards(): lax.psum(jnp.sum(mask_float * deviation * deviation), ('dp', 'expert'))  41.2 us
    psum x1, blocking collectives, shards(): lax.psum((router_part, value_part, loss_part), ('dp', 'expert'))  38.6 us
    psum x1, blocking collectives, shards(): lax.psum((jnp.sum(mask_float), jnp.sum(mask_float * returns)), ('dp', 'ex...  37.5 us
    unnamed x2, blocking collectives  32.7 us
    dot_general x1, matrix products, shards(): lax.dot_general(expert_rows, both_weights, last_last, preferred_element_t...  13.9 us
    dot_general x1, matrix products, shards(): lax.dot_general(both_delta, expert_rows, first_first, preferred_element_t...  13.1 us
  transfers between devices with their start and end apart: 5, of which 2 were waited for; matrix products, arithmetic and copies ran while one was open for 12% of the time, Pallas kernels for 0%

commit v1 on v0

--- a/solution.py
+++ b/solution.py
@@ -39,9 +39,9 @@
 
 def slot_numbers(block_routes, experts):
     flattened = block_routes.reshape(-1)
-    onehot = (flattened[:, None] == jnp.arange(experts, dtype=jnp.int32)[None, :]).astype(jnp.int32)
-    before = jnp.cumsum(onehot, axis=0) - onehot
-    return jnp.sum(before * onehot, axis=1).reshape(block_routes.shape)
+    place = jnp.arange(flattened.shape[0], dtype=jnp.int32)
+    same = (flattened[:, None] == flattened[None, :]) & (place[None, :] < place[:, None])
+    return jnp.sum(same.astype(jnp.int32), axis=1).reshape(block_routes.shape)
 
 
 def compose(earlier, later):

time: 435 us -> 434 us (level)
  no operation moved by 1% of the time
where the time goes in v1:
time: 434 us; the launch traced here: 433 us
  blocking collectives  233 us (54%)
  waiting for transfers between devices  53.5 us (12%)
  matrix products  43.6 us (10%)
  local copies, waits for them, and re-layouts  41.7 us (10%)
  between operations  21.5 us (5%)
  other arithmetic  18.5 us (4%)
  starting transfers between devices  12 us (3%)
  loops' own time  8.6 us (2%)
    all_to_all x1, blocking collectives, shards(): lax.all_to_all(outgoing, 'expert', split_axis=0, concat_axis=0, tiled=True)  77.9 us
    psum x1, waiting for transfers between devices, shards(): lax.psum((router_part, value_part, loss_part), ('dp', 'expert'))  52 us
    psum x1, blocking collectives, shards(): lax.psum(jnp.sum(mask_float * deviation * deviation), ('dp', 'expert'))  41.2 us
    psum x1, blocking collectives, shards(): lax.psum((router_part, value_part, loss_part), ('dp', 'expert'))  38.6 us
    psum x1, blocking collectives, shards(): lax.psum((jnp.sum(mask_float), jnp.sum(mask_float * returns)), ('dp', 'ex...  37.5 us
    unnamed x2, blocking collectives  32.7 us
    dot_general x1, matrix products, shards(): lax.dot_general(expert_rows, both_weights, last_last, preferred_element_t...  13.9 us
    dot_general x1, matrix products, shards(): lax.dot_general(both_delta, expert_rows, first_first, preferred_element_t...  13.1 us
  transfers between devices with their start and end apart: 5, of which 2 were waited for; matrix products, arithmetic and copies ran while one was open for 12% of the time, Pallas kernels for 0%

profile of v1, /device:TPU:0, one launch (start us, length us, event | category | flops | bytes accessed | tf_op | source)
XLA Modules:
  0.0 432.6 jit_solution(2480678895172874515)
XLA Ops:
  7.2 0.8 broadcast_multiply_fusion
  8.1 0.9 copy.40
  9.7 1.4 scatter_custom_fusion
  11.1 1.5 fusion.16
  12.7 2.5 fusion.18
  15.3 9.6 %gather_fusion = bf16[384,4096]{1,0:T(8,128)(2,1)} fusion(bf16[128,4096]{1,0:T(8,128)(2,1)} %fusion.18, s32[1024]{0:T(1024)S(1)} %pad_clamp_fusion.1), kind=kCustom, calls=%fused_computation | custom fusion | bytes 6292992 | tf_op jit(solution)/shard_map/jit(_take)/gather | solution.py:93
  24.8 2.2 broadcast_select_fusion
  27.0 77.9 %all_to_all.19 = bf16[8,48,4096]{2,1,0:T(8,128)(2,1)} all-to-all(bf16[8,48,4096]{2,1,0:T(8,128)(2,1)S(1)} %broadcast_select_fusion), channel_id=1, replica_groups=mesh['dp'=4,'expert'=8] {'expert'}, dimensions={0} | all-to-all | bytes 6291456 | tf_op jit(solution)/shard_map/all_to_all | solution.py:96
  106.8 1.3 collective-permute-start
  108.4 2.1 fusion.62
  110.6 1.4 gather_fusion.2
  114.3 2.6 fusion.60
  118.4 0.8 slice_dynamic-update-slice_fusion.1
  119.2 0.7 and_select_fusion.1
  119.9 0.7 slice_dynamic-update-slice_fusion
  121.2 21.6 %all-reduce.5 = (f32[8]{0:T(128)S(1)}, f32[8]{0:T(128)S(1)}) all-reduce(f32[8]{0:T(128)S(1)} %slice_dynamic-update-slice_fusion.1, f32[8]{0:T(128)S(1)} %slice_dynamic-update-slice_fusion), channel_id=1, replica_groups=mesh['dp'=4,'expert'=8] {'expert'}, use_global_device_ids=true, to_apply=%add | all-reduce | flops 16 | bytes 128
  142.8 17.1 %while.14 = (s32[]{:T(128)}, f32[]{:T(128)}, s32[]{:T(128)}, f32[8]{0:T(128)S(1)}, f32[8]{0:T(128)S(1)}, /*index=5*/s32[]{:T(128)}, s32[]{:T(128)}, s32[]{:T(128)}, s32[]{:T(128)}) while((s32[]{:T(128)}, f32[]{:T(128)}, s32[]{:T(128)}, f32[8]{0:T(128)S(1)}, f32[8]{0:T(128)S(1)}, /*index=5*/s32[]{:T(128)}, s32[]{:T(128)}, s32[]{:T(128)}, ...), condition=%wide.region_8.9_spmd, body=%wide.region_7.8_spmd.sunk | while | flops 8 | bytes 195 | solution.py:31
  147.7 0.7 dynamic_slice.17
  159.9 1.3 fusion.51
  161.1 37.5 %all-reduce.4 = (f32[]{:T(128)}, f32[]{:T(128)}) all-reduce(f32[]{:T(128)} %get-tuple-element.110, f32[]{:T(128)} %convert_reduce_fusion.1), channel_id=1, replica_groups=mesh['dp'=4,'expert'=8] {'dp','expert'}, use_global_device_ids=true, to_apply=%region_10.11 | all-reduce | flops 2 | bytes 16 | tf_op jit(solution)/shard_map/psum | solution.py:139
  199.9 13.9 %fusion = f32[1536,768]{0,1:T(8,128)S(1)} fusion(bf16[1536,4096]{1,0:T(8,128)(2,1)} %bitcast.118, bf16[384,4096]{1,0:T(8,128)(2,1)} %bitcast.120, bf16[384,4096]{1,0:T(8,128)(2,1)} %bitcast.121), kind=kOutput, calls=%fused_computation.6 | convolution fusion | flops 9676259328 | bytes 23592960 | tf_op jit(solution)/shard_map/dot_general | solution.py:99
  213.8 2.1 copy-done.1
  215.9 0.7 multiply_convert_fusion.1
  216.7 1.0 copy-done.2
  218.4 11.1 %all-reduce.2 = f32[4,8,48]{2,1,0:T(8,128)S(1)} all-reduce(f32[4,8,48]{2,1,0:T(8,128)S(1)} %reshape.259), channel_id=4, replica_groups=mesh['dp'=4,'expert'=8] {'dp'}, use_global_device_ids=true, to_apply=%region_4.5.clone | all-reduce | flops 1536 | bytes 12288
  229.5 1.2 constant_dynamic-slice_fusion
  230.7 5.1 %all-to-all-start.1 = ((f32[1,8,48]{2,0,1:T(1,128)}), f32[1,8,48]{2,0,1:T(1,128)S(1)}, u32[]{:S(2)}, u32[]{:S(2)}) async-start(f32[1,8,48]{2,0,1:T(1,128)} %bitcast.15), calls=%async_computation.1 | async-start | bytes 8192 | tf_op jit(solution)/shard_map/all_to_all | solution.py:111
  236.7 41.2 %psum.44 = f32[]{:T(128)} all-reduce(f32[]{:T(128)} %fusion.46), channel_id=1, replica_groups=mesh['dp'=4,'expert'=8] {'dp','expert'}, use_global_device_ids=true, to_apply=%region_14.15 | all-reduce | flops 1 | bytes 8 | tf_op jit(solution)/shard_map/psum | solution.py:145
  279.0 0.7 reduce.13
  279.8 1.9 gather_fusion.1
  282.0 3.3 multiply_reduce_fusion.2
  285.5 1.4 scatter_custom_fusion.1
  286.9 0.7 all_to_all.14
  287.6 5.5 %all-to-all-start.2 = ((f32[8,1,48]{2,1,0:T(1,128)}), f32[8,1,48]{2,1,0:T(1,128)S(1)}, u32[]{:S(2)}, u32[]{:S(2)}) async-start(f32[8,1,48]{2,1,0:T(1,128)} %all_to_all.14), calls=%async_computation.2 | async-start | bytes 8192 | tf_op jit(solution)/shard_map/all_to_all | solution.py:158
  293.2 2.4 fusion.63
  295.6 1.7 fusion.20
  298.0 1.5 all-to-all-done.2
  299.5 5.4 %all-gather.1 = f32[32,1,48]{2,1,0:T(1,128)S(1)} all-gather(f32[8,1,48]{2,1,0:T(1,128)S(1)} %all-to-all-done.2), channel_id=3, replica_groups=mesh['dp'=4,'expert'=8] {'dp'}, dimensions={0}, use_global_device_ids=true | all-gather | bytes 7680 | tf_op jit(solution)/shard_map/all_gather | solution.py:159
  304.9 0.7 reduce.14
  305.7 2.3 fusion.61
  308.0 1.3 fusion.4
  309.4 3.5 fusion.10
  312.9 13.1 %convolution_convert_fusion = bf16[768,4096]{1,0:T(8,128)(2,1)S(1)} fusion(bf16[1536,4096]{1,0:T(8,128)(2,1)} %bitcast.119, bf16[1536,384]{0,1:T(8,128)(2,1)S(1)} %get-tuple-element.119, bf16[1536,384]{0,1:T(8,128)(2,1)S(1)} %get-tuple-element.118), kind=kOutput, calls=%fused_computation.5 | convolution fusion | flops 9671540736 | bytes 21233664 | tf_op jit(solution)/shard_map/dot_general | solution.py:169
  326.0 3.5 slice_bitcast_fusion
  329.5 2.3 multiply_convert_fusion
  331.8 38.6 %all-reduce.3 = (f32[]{:T(128)}, f32[4096]{0:T(1024)}) all-reduce(f32[]{:T(128)S(6)} %mul_shard_map.3, f32[4096]{0:T(1024)S(1)} %add.167), channel_id=1, replica_groups=mesh['dp'=4,'expert'=8] {'dp','expert'}, use_global_device_ids=true, to_apply=%region_16.17 | all-reduce | flops 4097 | bytes 32776 | tf_op jit(solution)/shard_map/psum | solution.py:186
  371.1 52.0 %all-reduce.8.cloned.1.call-done = f32[8,4096]{1,0:T(8,128)} async-done(((f32[8,4096]{1,0:T(8,128)}), f32[8,4096]{1,0:T(8,128)}) %all-reduce.8.cloned.1.call-update) | async-done | bytes 131088 | tf_op jit(solution)/shard_map/psum | solution.py:186
  423.0 1.6 copy.59
  (89 shorter events, 15.5 us)
Async XLA Ops:
  7.2 107.1 %copy-start = (bf16[1,384,4096]{2,1,0:T(8,128)(2,1)S(1)}, bf16[1,384,4096]{2,1,0:T(8,128)(2,1)}, u32[]{:S(2)}) copy-start(bf16[1,384,4096]{2,1,0:T(8,128)(2,1)} %param.20) | copy-start | bytes 9437188
  7.2 192.7 %all-gather.4.cloned.1.call-start = ((), (), s32[]{:S(2)}) async-start(), calls=%async_computation.4 | async-start | bytes 15728640 | tf_op jit(solution)/shard_map/all_gather | solution.py:97
  104.9 0.7 copy-start.6
  104.9 3.2 copy-start.5
  104.9 3.5 copy-start.4
  106.8 10.1 %collective-permute-start = (s32[1]{0:T(128)}, s32[1]{0:T(128)}, u32[]{:S(2)}, u32[]{:S(2)}) collective-permute-start(s32[1]{0:T(128)} %bitcast.21), channel_id=1, source_target_pairs={{1,0},{2,1},{3,2},{4,3},{5,4},{6,5},{7,6},{9,8},{10,9},{11,10},{12... | collective-permute-start | bytes 20 | tf_op jit(solution)/shard_map/ppermute | solution.py:15
  110.5 2.3 copy-start.11
  110.5 2.9 copy-start.7
  110.5 3.6 copy-start.8
  110.6 3.7 copy-start.3
  112.0 6.2 %copy-start.9 = (f32[1,128]{1,0:T(1,128)S(1)}, f32[1,128]{1,0:T(1,128)}, u32[]{:S(2)}) copy-start(f32[1,128]{1,0:T(1,128)} %param.24) | copy-start | bytes 1540
  112.0 8.7 %copy-start.10 = (u32[32]{0:T(128)S(1)}, u32[32]{0:T(128)}, u32[]{:S(2)}) copy-start(u32[32]{0:T(128)} %constant.138) | copy-start | bytes 388
  213.8 2.1 copy-start.1
  216.7 1.0 copy-start.2
  230.7 47.8 %all-to-all-start.1 = ((f32[1,8,48]{2,0,1:T(1,128)}), f32[1,8,48]{2,0,1:T(1,128)S(1)}, u32[]{:S(2)}, u32[]{:S(2)}) async-start(f32[1,8,48]{2,0,1:T(1,128)} %bitcast.15), calls=%async_computation.1 | async-start | bytes 8192 | tf_op jit(solution)/shard_map/all_to_all | solution.py:111
  287.6 11.9 %all-to-all-start.2 = ((f32[8,1,48]{2,1,0:T(1,128)}), f32[8,1,48]{2,1,0:T(1,128)S(1)}, u32[]{:S(2)}, u32[]{:S(2)}) async-start(f32[8,1,48]{2,1,0:T(1,128)} %all_to_all.14), calls=%async_computation.2 | async-start | bytes 8192 | tf_op jit(solution)/shard_map/all_to_all | solution.py:158
  293.1 129.9 %all-reduce.8.cloned.1.call-start = ((), (), s32[]{:S(2)}) async-start(), calls=%async_computation.3 | async-start | bytes 262144 | tf_op jit(solution)/shard_map/psum | solution.py:186
Sparse Core Ops, SparseCore 0:
  105.1 81.7 all-gather.3
  300.1 122.9 all-reduce.7

commit v2 on v1

v2 whole, which is shorter than its diff:
```python
import functools

import jax
import jax.numpy as jnp
from jax import lax
from jax.sharding import PartitionSpec as P

discount_rate = 0.9995
norm_epsilon = 1e-06
white_epsilon = 1e-05
highest = lax.Precision.HIGHEST


def norm_rows(tokens, norm_gain):
    as_float = tokens.astype(jnp.float32)
    inverse_rms = lax.rsqrt(jnp.mean(as_float * as_float, axis=-1, keepdims=True) + norm_epsilon)
    return (as_float * inverse_rms * norm_gain).astype(jnp.bfloat16)


def slot_numbers(block_routes, experts):
    flattened = block_routes.reshape(-1)
    place = jnp.arange(flattened.shape[0], dtype=jnp.int32)
    same = (flattened[:, None] == flattened[None, :]) & (place[None, :] < place[:, None])
    return jnp.sum(same.astype(jnp.int32), axis=1).reshape(block_routes.shape)


def shifted_back(array, by, fill):
    return jnp.concatenate(
        [array[:, by:], jnp.full((array.shape[0], by), fill, array.dtype)], axis=1
    )


def row_returns(reward, same_next):
    total, factor, by = reward, discount_rate * same_next, 1
    while by < reward.shape[1]:
        total = total + factor * shifted_back(total, by, 0.0)
        factor = factor * shifted_back(factor, by, 0.0)
        by *= 2
    return total


def expert_block(outgoing):
    incoming = lax.all_to_all(outgoing, "expert", split_axis=0, concat_axis=0, tiled=True)
    return lax.all_gather(incoming[None], "dp", axis=0, tiled=True)


def shards(
    tokens,
    norm_gain,
    router_weight,
    value_weight,
    gate_weight,
    up_weight,
    down_weight,
    routes,
    segment_ids,
    loss_mask,
    penalty_reward,
    scores,
):
    tok_count = tokens.shape[1]
    model_width = tokens.shape[2]
    route_count = routes.shape[2]
    experts = router_weight.shape[0]
    dp_count = lax.axis_size("dp")
    expert_count = lax.axis_size("expert")
    devices = dp_count * expert_count
    both = ("dp", "expert")
    me = lax.axis_index("dp") * expert_count + lax.axis_index("expert")
    capacity = tok_count * route_count * 3 // (2 * experts)
    last_last = (((1,), (1,)), ((), ()))
    first_first = (((0,), (0,)), ((), ()))
    own_tokens = tokens[0]
    own_routes = routes[0]
    mask_float = loss_mask[0].astype(jnp.float32)

    segment = segment_ids[0]
    segment_hit = segment[:, None] == jnp.arange(scores.shape[1], dtype=jnp.int32)[None, :]
    score_pick = jnp.sum(jnp.where(segment_hit, scores[0][None, :], 0.0), axis=1)
    small = jnp.stack([segment.astype(jnp.float32), mask_float, penalty_reward[0], score_pick])
    small = lax.all_gather(small, both, axis=0, tiled=False)
    small = jnp.transpose(small, (1, 0, 2)).reshape(4, dp_count, expert_count * tok_count)

    normed = norm_rows(own_tokens, norm_gain)
    slot_number = slot_numbers(own_routes, experts)
    slot_place = own_routes * capacity + slot_number
    slots = jnp.arange(experts * capacity, dtype=jnp.int32)
    hits = [slots[:, None] == slot_place[:, k][None, :] for k in range(route_count)]
    pick = functools.reduce(jnp.logical_or, hits).astype(jnp.bfloat16)
    outgoing = jnp.dot(pick, normed, preferred_element_type=jnp.float32).astype(jnp.bfloat16)
    outgoing = outgoing.reshape(experts, capacity, model_width)
    expert_rows = expert_block(outgoing).reshape(-1, model_width)

    normed_float = normed.astype(jnp.float32)
    logits = lax.dot_general(normed_float, router_weight, last_last, precision=highest)
    expert_hit = own_routes[:, :, None] == jnp.arange(experts, dtype=jnp.int32)[None, None, :]
    chosen = jnp.sum(jnp.where(expert_hit, logits[:, None, :], 0.0), axis=2)
    gate_sigmoid = jax.nn.sigmoid(chosen)
    sigmoid_total = jnp.sum(gate_sigmoid, axis=1, keepdims=True)
    route_prob = gate_sigmoid / sigmoid_total

    segments, masks, penalties, picks = small
    same_next = (shifted_back(segments, 1, -1.0) == segments).astype(jnp.float32)
    returns = row_returns(penalties + jnp.where(same_next > 0.0, 0.0, picks), same_next)
    divisor = jnp.maximum(jnp.sum(masks), 1.0)
    centre = jnp.sum(masks * returns) / divisor
    deviation = returns - centre
    variance = jnp.sum(masks * deviation * deviation) / divisor
    whitened = deviation * lax.rsqrt(variance + white_epsilon)
    whitened = lax.dynamic_index_in_dim(whitened.reshape(devices, tok_count), me, 0, False)

    down_float = down_weight[0].astype(jnp.float32)
    value_along = jnp.dot(down_float, value_weight, precision=highest)
    own_head = jnp.dot(own_tokens.astype(jnp.float32), value_weight, precision=highest)

    gate_value = lax.dot_general(
        expert_rows, gate_weight[0], last_last, preferred_element_type=jnp.float32
    )
    up_value = lax.dot_general(
        expert_rows, up_weight[0], last_last, preferred_element_type=jnp.float32
    )
    gate_sig = jax.nn.sigmoid(gate_value)
    hidden = (gate_value * gate_sig * up_value).astype(jnp.bfloat16)
    partial_value = jnp.sum(hidden.astype(jnp.float32) * value_along[None, :], axis=1)
    returned = lax.all_to_all(
        partial_value.reshape(devices, capacity), both, split_axis=0, concat_axis=0, tiled=True
    )
    returned = jnp.sum(returned.reshape(dp_count, expert_count * capacity), axis=0)
    route_value = jnp.stack(
        [jnp.sum(jnp.where(hit, returned[:, None], 0.0), axis=0) for hit in hits], axis=1
    )
    own_values = own_head + jnp.sum(route_prob * route_value, axis=1)
    value_error = mask_float * (own_values - whitened)
    loss_part = 0.5 * jnp.sum(mask_float * (own_values - whitened) * (own_values - whitened))
    route_weight = value_error[:, None] * route_prob
    prob_grad = value_error[:, None] * route_value
    weight_table = sum(
        jnp.sum(jnp.where(hit, route_weight[:, k][None, :], 0.0), axis=1)
        for k, hit in enumerate(hits)
    ).reshape(1, experts, capacity)
    weight_table = jnp.broadcast_to(weight_table, (dp_count, experts, capacity))
    row_weight = lax.all_to_all(
        weight_table.reshape(devices, capacity), both, split_axis=0, concat_axis=0, tiled=True
    ).reshape(-1)
    spread = jnp.sum(row_weight[:, None] * hidden.astype(jnp.float32), axis=0)
    down_grad = (spread[:, None] * value_weight[None, :]).astype(jnp.bfloat16)
    hidden_grad = row_weight[:, None] * value_along[None, :]
    gate_delta = (hidden_grad * up_value * gate_sig * (1.0 + gate_value * (1.0 - gate_sig))).astype(
        jnp.bfloat16
    )
    up_delta = (hidden_grad * gate_value * gate_sig).astype(jnp.bfloat16)
    sigma_grad = (
        prob_grad - jnp.sum(prob_grad * route_prob, axis=1, keepdims=True)
    ) / sigmoid_total
    chosen_grad = sigma_grad * gate_sigmoid * (1.0 - gate_sigmoid)
    logit_grad = jnp.sum(jnp.where(expert_hit, chosen_grad[:, :, None], 0.0), axis=1)
    router_part = lax.dot_general(logit_grad, normed_float, first_first, precision=highest)
    value_part = jnp.dot(value_error, own_tokens.astype(jnp.float32), precision=highest) + jnp.dot(
        spread, down_float, precision=highest
    )
    parts = jnp.concatenate(
        [router_part, value_part[None], jnp.full((1, model_width), loss_part)], axis=0
    )
    parts = jnp.transpose(parts.reshape(experts + 2, devices, -1), (1, 0, 2))
    parts = lax.all_to_all(parts, both, split_axis=0, concat_axis=0, tiled=True)
    totals = lax.all_gather(jnp.sum(parts, axis=0), both, axis=0, tiled=False)
    totals = jnp.transpose(totals, (1, 0, 2)).reshape(experts + 2, model_width)
    gate_grad = lax.dot_general(
        gate_delta, expert_rows, first_first, preferred_element_type=jnp.float32
    ).astype(jnp.bfloat16)
    up_grad = lax.dot_general(
        up_delta, expert_rows, first_first, preferred_element_type=jnp.float32
    ).astype(jnp.bfloat16)
    return (
        own_values[None],
        totals[experts + 1, 0] / divisor,
        totals[experts],
        totals[:experts],
        gate_grad[None],
        up_grad[None],
        down_grad[None],
    )


def solution(mesh):
    placed = (
        P("dp", "expert", None),
        P(),
        P(),
        P(),
        P("expert", "dp", None),
        P("expert", "dp", None),
        P("expert", "dp", None),
        P("dp", "expert", None),
        P("dp", "expert"),
        P("dp", "expert"),
        P("dp", "expert"),
        P("dp", None),
    )
    return jax.shard_map(
        shards,
        mesh=mesh,
        in_specs=placed,
        out_specs=(
            P("dp", "expert"),
            P(),
            P(),
            P(),
            P("expert", "dp", None),
            P("expert", "dp", None),
            P("expert", "dp", None),
        ),
        check_vma=False,
    )
```

time: 434 us -> 332 us (0.76)
  waiting for transfers between devices: 53.5 us -> 6.96 us
  local copies, waits for them, and re-layouts: 41.7 us -> 9.62 us
  blocking collectives: 233 us -> 215 us
  matrix products: 43.6 us -> 59.4 us
  loops' own time: 8.6 us -> 0 us
  other arithmetic: 18.5 us -> 10.8 us
    all_gather x1 -> x2, blocking collectives: 5.39 us -> 137 us  [the longest x1 70.1 us: shards(): totals = lax.all_gather(jnp.sum(parts, axis=0), both, axis=0, tiled=False)]
    psum x3 -> x0, blocking collectives: 117 us -> none  [the longest x1 41.2 us: shards(): lax.psum(jnp.sum(mask_float * deviation * deviation), ('dp', 'expert'))]
    psum x1 -> x0, waiting for transfers between devices: 52 us -> none  [shards(): lax.psum((router_part, value_part, loss_part), ('dp', 'expert'))]
    unnamed x2 -> x0, blocking collectives: 32.7 us -> none
    dot_general x7, matrix products: 34.6 us -> 48.6 us  [the longest x1 11.3 us: shards(): lax.dot_general(gate_delta, expert_rows, first_first, preferred_element_t...]
    gather x7 -> x0, local copies, waits for them, and re-layouts: 13.4 us -> none  [the longest x1 9.6 us: shards(): jnp.take(normed, source_index, axis=0, mode='fill', fill_value=0)]
    another operation x1 -> x0, loops' own time: 8.6 us -> none  [entering(): return lax.fori_loop(0, ahead, one, state)]
    unnamed x33 -> x27, local copies, waits for them, and re-layouts: 10.2 us -> 1.65 us
  transfers between devices with their start and end apart: 5 -> 4, of which waited for: 2 -> 2; matrix products, arithmetic and copies ran while one was open for 12% -> 10% of each run, Pallas kernels for 0% -> 0%
where the time goes in v2:
time: 332 us; the launch traced here: 331 us
  blocking collectives  215 us (65%)
  matrix products  59.4 us (18%)
  between operations  18.9 us (6%)
  other arithmetic  10.8 us (3%)
  starting transfers between devices  10.3 us (3%)
  local copies, waits for them, and re-layouts  9.62 us (3%)
  waiting for transfers between devices  6.96 us (2%)
    all_to_all x1, blocking collectives, expert_block(): lax.all_to_all(outgoing, 'expert', split_axis=0, concat_axis=0, tiled=True)  77.9 us
    all_gather x1, blocking collectives, shards(): totals = lax.all_gather(jnp.sum(parts, axis=0), both, axis=0, tiled=False)  70.1 us
    all_gather x1, blocking collectives, shards(): small = lax.all_gather(small, both, axis=0, tiled=False)  67.4 us
    dot_general x1, matrix products, shards(): lax.dot_general(gate_delta, expert_rows, first_first, preferred_element_t...  11.3 us
    dot_general x1, matrix products, shards(): lax.dot_general(expert_rows, gate_weight[0], last_last, preferred_element...  10.9 us
    dot_general x1, matrix products, shards(): lax.dot_general(up_delta, expert_rows, first_first, preferred_element_typ...  10.7 us
    dot_general x1, matrix products, shards(): lax.dot_general(expert_rows, up_weight[0], last_last, preferred_element_t...  8.89 us
  transfers between devices with their start and end apart: 4, of which 2 were waited for; matrix products, arithmetic and copies ran while one was open for 10% of the time, Pallas kernels for 0%

profile of v2, /device:TPU:0, one launch (start us, length us, event | category | flops | bytes accessed | tf_op | source)
XLA Modules:
  0.0 331.3 jit_solution(1430613771494066951)
XLA Ops:
  7.2 1.7 fusion.17
  8.9 0.8 copy.44
  9.7 0.1 eq.83
  9.8 0.2 convert_reduce_fusion
  10.0 0.1 reshape.211
  10.2 0.2 slice_reduce_fusion.1
  10.4 2.3 convolution_convert_fusion.2
  12.7 77.9 %all_to_all.28 = bf16[8,48,4096]{2,1,0:T(8,128)(2,1)} all-to-all(bf16[8,48,4096]{2,1,0:T(8,128)(2,1)S(1)} %bitcast.99), channel_id=1, replica_groups=mesh['dp'=4,'expert'=8] {'expert'}, dimensions={0} | all-to-all | bytes 6291456 | tf_op jit(solution)/shard_map/all_to_all | solution.py:43
  90.6 0.6 copy-done.10
  91.2 0.1 select_reduce_fusion.6
  91.3 67.4 %all-gather.3 = f32[32,4,128]{2,1,0:T(4,128)S(1)} all-gather(f32[1,4,128]{2,1,0:T(4,128)S(1)} %maximum_bitcast_fusion.1), channel_id=3, replica_groups=mesh['dp'=4,'expert'=8] {'dp','expert'}, dimensions={0}, use_global_device_ids=true | all-gather | bytes 67584 | tf_op jit(solution)/shard_map/all_gather | solution.py:81
  158.7 0.8 slice_reduce_fusion.5
  161.6 0.6 multiply_reduce_fusion
  162.9 0.6 fusion.40
  164.3 2.3 fusion.50
  166.6 4.4 %fusion.28 = f32[384]{0:T(512)S(1)} fusion(f32[4096,1]{0,1:T(1,128)S(1)} %bitcast.108, bf16[1,384,4096]{2,1,0:T(8,128)(2,1)} %param.18), kind=kOutput, calls=%fused_computation.38 | convolution fusion | flops 18874368 | bytes 3163648 | tf_op jit(solution)/shard_map/dot_general | solution.py:113
  171.1 1.3 fusion.48
  172.4 10.9 %fusion.8 = f32[1536,384]{1,0:T(8,128)S(1)} fusion(bf16[1536,4096]{1,0:T(8,128)(2,1)} %bitcast.123, bf16[1,384,4096]{2,1,0:T(8,128)(2,1)} %param.16), kind=kOutput, calls=%fused_computation.14 | convolution fusion | flops 4831838208 | bytes 18087936 | tf_op jit(solution)/shard_map/dot_general | solution.py:116
  183.3 8.9 %fusion.10 = (f32[1536]{0:T(1024)S(1)}, bf16[1536,384]{1,0:T(8,128)(2,1)}, f32[1536,384]{1,0:T(8,128)}) fusion(f32[384]{0:T(512)S(1)} %fusion.28, f32[1536,384]{1,0:T(8,128)S(1)} %fusion.8, bf16[1536,4096]{1,0:T(8,128)(2,1)S(1)} %bitcast.126, bf16[1,384,4096]{2,1,0:T(8,128)(2,1)S(1)} %copy-done), kind=kOutput, calls=%fused_computation.20 | convolution fusion | flops 4837145088 | bytes 21634560 | tf_op jit(solution)/shard_map/dot_general | solution.py:119
  192.2 0.7 all_to_all.19
  192.9 4.3 %all-to-all-start.1 = ((f32[32,1,48]{2,1,0:T(1,128)}), f32[32,1,48]{2,1,0:T(1,128)S(1)}, u32[]{:S(2)}, u32[]{:S(2)}) async-start(f32[32,1,48]{2,1,0:T(1,128)} %all_to_all.19), calls=%async_computation.1 | async-start | bytes 32768 | tf_op jit(solution)/shard_map/all_to_all | solution.py:125
  197.3 2.3 copy.49
  199.6 4.5 %all-to-all-done.1 = f32[32,1,48]{2,1,0:T(1,128)S(1)} async-done(((f32[32,1,48]{2,1,0:T(1,128)}), f32[32,1,48]{2,1,0:T(1,128)S(1)}, u32[]{:S(2)}, u32[]{:S(2)}) %all-to-all-start.1) | async-done | bytes 6176 | tf_op jit(solution)/shard_map/all_to_all | solution.py:125
  204.1 0.5 broadcast.206
  204.6 0.7 reduce.29
  205.3 0.1 reshape.214
  205.4 0.1 select_reduce_fusion.3
  205.6 3.3 multiply_reduce_fusion.3
  208.9 0.2 select_reduce_fusion
  209.1 0.1 add.147
  209.2 0.6 broadcast_in_dim.131
  209.8 2.5 all-to-all-start.2
  212.4 2.1 fusion.41
  214.5 1.8 fusion.32
  217.0 2.4 all-to-all-done.2
  219.4 0.7 reduce.30
  220.2 10.7 %fusion.1 = bf16[1,384,4096]{2,1,0:T(8,128)(2,1)} fusion(bf16[1536,4096]{1,0:T(8,128)(2,1)} %bitcast.124, f32[1536,384]{1,0:T(8,128)} %copy-done.11, f32[1536]{0:T(1024)S(1)} %mul.268, f32[384]{0:T(512)S(1)} %fusion.28), kind=kOutput, calls=%fused_computation.5 | convolution fusion | flops 4837539840 | bytes 18095616 | tf_op jit(solution)/shard_map/dot_general | solution.py:171
  230.9 0.3 fusion.11
  231.3 1.3 fusion.2
  232.6 0.8 maximum_bitcast_fusion
  233.4 3.4 %all-to-all-start.3 = ((f32[32,10,128]{2,1,0:T(8,128)}), f32[32,10,128]{2,1,0:T(8,128)S(1)}, u32[]{:S(2)}, u32[]{:S(2)}) async-start(f32[32,10,128]{2,1,0:T(8,128)} %maximum_bitcast_fusion), calls=%async_computation.3 | async-start | bytes 524288 | tf_op jit(solution)/shard_map/all_to_all | solution.py:165
  236.8 11.3 %fusion = bf16[1,384,4096]{2,1,0:T(8,128)(2,1)} fusion(bf16[1536,4096]{1,0:T(8,128)(2,1)} %bitcast.125, f32[1536,384]{1,0:T(8,128)} %get-tuple-element.46, f32[1536,384]{1,0:T(8,128)} %copy-done.11, f32[1536]{0:T(1024)S(1)} %mul.268, f32[384]{0:T(512)S(1)} %fusion.28), kind=kOutput, calls=%fused_computation.4 | convolution fusion | flops 4839899136 | bytes 20454912 | tf_op jit(solution)/shard_map/dot_general | solution.py:168
  248.2 2.3 multiply_convert_fusion
  250.5 70.1 %all-gather.4 = f32[32,10,128]{2,1,0:T(8,128)S(1)} all-gather(f32[1,10,128]{2,1,0:T(8,128)S(1)} %bitcast.113), channel_id=4, replica_groups=mesh['dp'=4,'expert'=8] {'dp','expert'}, dimensions={0}, use_global_device_ids=true | all-gather | bytes 168960 | tf_op jit(solution)/shard_map/all_gather | solution.py:166
  320.6 0.6 slice.140
  321.2 0.7 slice_bitcast_fusion
  322.0 0.2 copy.50
  322.1 0.5 slice.139
  (86 shorter events, 2.0 us)
Async XLA Ops:
  7.2 176.2 %copy-start = (bf16[1,384,4096]{2,1,0:T(8,128)(2,1)S(1)}, bf16[1,384,4096]{2,1,0:T(8,128)(2,1)}, u32[]{:S(2)}) copy-start(bf16[1,384,4096]{2,1,0:T(8,128)(2,1)} %param.17) | copy-start | bytes 9437188
  7.2 165.2 %all-gather.7.cloned.1.call-start = ((), (), s32[]{:S(2)}) async-start(), calls=%async_computation.4 | async-start | bytes 15728640 | tf_op jit(solution)/shard_map/all_gather | solution.py:44
  90.6 0.7 copy-start.10
  90.6 0.7 copy-start.6
  90.6 0.7 copy-start.9
  90.6 0.8 copy-start.7
  90.6 73.7 %copy-start.5 = (f32[4096]{0:T(1024)S(1)}, f32[4096]{0:T(1024)}, u32[]{:S(2)}) copy-start(f32[4096]{0:T(1024)} %param.13) | copy-start | bytes 49156
  91.2 75.4 %copy-start.4 = (f32[4096]{0:T(1024)S(1)}, f32[4096]{0:T(1024)}, u32[]{:S(2)}) copy-start(f32[4096]{0:T(1024)} %param.15) | copy-start | bytes 49156
  164.3 6.8 %copy-start.1 = (bf16[1,128,4096]{2,1,0:T(8,128)(2,1)S(1)}, bf16[1,128,4096]{2,1,0:T(8,128)(2,1)}, u32[]{:S(2)}) copy-start(bf16[1,128,4096]{2,1,0:T(8,128)(2,1)} %param.12) | copy-start | bytes 3145732
  172.4 10.9 %copy-start.8 = (bf16[32,48,4096]{2,1,0:T(8,128)(2,1)S(1)}, bf16[32,48,4096]{2,1,0:T(8,128)(2,1)}, u32[]{:S(2)}) copy-start(bf16[32,48,4096]{2,1,0:T(8,128)(2,1)} %all-gather.7.cloned.1.call-done) | copy-start | bytes 37748740
  183.3 8.9 %copy-start.11 = (f32[1536,384]{1,0:T(8,128)}, f32[1536,384]{1,0:T(8,128)S(1)}, u32[]{:S(2)}) copy-start(f32[1536,384]{1,0:T(8,128)S(1)} %fusion.8) | copy-start | bytes 7077892
  192.9 11.1 %all-to-all-start.1 = ((f32[32,1,48]{2,1,0:T(1,128)}), f32[32,1,48]{2,1,0:T(1,128)S(1)}, u32[]{:S(2)}, u32[]{:S(2)}) async-start(f32[32,1,48]{2,1,0:T(1,128)} %all_to_all.19), calls=%async_computation.1 | async-start | bytes 32768 | tf_op jit(solution)/shard_map/all_to_all | solution.py:125
  209.8 9.6 %all-to-all-start.2 = ((f32[32,1,48]{2,1,0:T(1,128)}), f32[32,1,48]{2,1,0:T(1,128)S(1)}, u32[]{:S(2)}, u32[]{:S(2)}) async-start(f32[32,1,48]{2,1,0:T(1,128)} %bitcast.27), calls=%async_computation.2 | async-start | bytes 32768 | tf_op jit(solution)/shard_map/all_to_all | solution.py:142
  220.2 10.7 %copy-start.3 = (bf16[1536,384]{1,0:T(8,128)(2,1)S(1)}, bf16[1536,384]{1,0:T(8,128)(2,1)}, u32[]{:S(2)}) copy-start(bf16[1536,384]{1,0:T(8,128)(2,1)} %get-tuple-element.41) | copy-start | bytes 3538948
  220.2 11.1 %copy-start.2 = (bf16[1,384,4096]{2,1,0:T(8,128)(2,1)S(1)}, bf16[1,384,4096]{2,1,0:T(8,128)(2,1)}, u32[]{:S(2)}) copy-start(bf16[1,384,4096]{2,1,0:T(8,128)(2,1)} %param.18) | copy-start | bytes 9437188
  233.4 17.1 %all-to-all-start.3 = ((f32[32,10,128]{2,1,0:T(8,128)}), f32[32,10,128]{2,1,0:T(8,128)S(1)}, u32[]{:S(2)}, u32[]{:S(2)}) async-start(f32[32,10,128]{2,1,0:T(8,128)} %maximum_bitcast_fusion), calls=%async_computation.3 | async-start | bytes 524288 | tf_op jit(solution)/shard_map/all_to_all | solution.py:165
Sparse Core Ops, SparseCore 0:
  90.7 81.0 all-gather.6

commit v3 on v2

--- a/solution.py
+++ b/solution.py
@@ -37,6 +37,12 @@
         factor = factor * shifted_back(factor, by, 0.0)
         by *= 2
     return total
+
+
+def to_all(array, axes):
+    count = lax.axis_size(axes[0]) * lax.axis_size(axes[1])
+    copies = jnp.broadcast_to(array[None], (count, *array.shape))
+    return lax.all_to_all(copies, axes, split_axis=0, concat_axis=0, tiled=True)
 
 
 def expert_block(outgoing):
@@ -78,7 +84,7 @@
     segment_hit = segment[:, None] == jnp.arange(scores.shape[1], dtype=jnp.int32)[None, :]
     score_pick = jnp.sum(jnp.where(segment_hit, scores[0][None, :], 0.0), axis=1)
     small = jnp.stack([segment.astype(jnp.float32), mask_float, penalty_reward[0], score_pick])
-    small = lax.all_gather(small, both, axis=0, tiled=False)
+    small = to_all(small, both)
     small = jnp.transpose(small, (1, 0, 2)).reshape(4, dp_count, expert_count * tok_count)
 
     normed = norm_rows(own_tokens, norm_gain)
@@ -89,7 +95,12 @@
     pick = functools.reduce(jnp.logical_or, hits).astype(jnp.bfloat16)
     outgoing = jnp.dot(pick, normed, preferred_element_type=jnp.float32).astype(jnp.bfloat16)
     outgoing = outgoing.reshape(experts, capacity, model_width)
-    expert_rows = expert_block(outgoing).reshape(-1, model_width)
+    chunks = max(capacity // 16, 1)
+    chunk = capacity // chunks
+    row_chunks = [
+        expert_block(outgoing[:, c * chunk : (c + 1) * chunk]).reshape(-1, model_width)
+        for c in range(chunks)
+    ]
 
     normed_float = normed.astype(jnp.float32)
     logits = lax.dot_general(normed_float, router_weight, last_last, precision=highest)
@@ -113,17 +124,22 @@
     value_along = jnp.dot(down_float, value_weight, precision=highest)
     own_head = jnp.dot(own_tokens.astype(jnp.float32), value_weight, precision=highest)
 
-    gate_value = lax.dot_general(
-        expert_rows, gate_weight[0], last_last, preferred_element_type=jnp.float32
-    )
-    up_value = lax.dot_general(
-        expert_rows, up_weight[0], last_last, preferred_element_type=jnp.float32
-    )
-    gate_sig = jax.nn.sigmoid(gate_value)
-    hidden = (gate_value * gate_sig * up_value).astype(jnp.bfloat16)
-    partial_value = jnp.sum(hidden.astype(jnp.float32) * value_along[None, :], axis=1)
+    kept, partial_values = [], []
+    for rows in row_chunks:
+        gate_value = lax.dot_general(
+            rows, gate_weight[0], last_last, preferred_element_type=jnp.float32
+        )
+        up_value = lax.dot_general(
+            rows, up_weight[0], last_last, preferred_element_type=jnp.float32
+        )
+        gate_sig = jax.nn.sigmoid(gate_value)
+        hidden = (gate_value * gate_sig * up_value).astype(jnp.bfloat16)
+        partial = jnp.sum(hidden.astype(jnp.float32) * value_along[None, :], axis=1)
+        partial_values.append(partial.reshape(devices, chunk))
+        kept.append((gate_value, up_value, gate_sig, hidden))
+    partial_value = jnp.concatenate(partial_values, axis=1)
     returned = lax.all_to_all(
-        partial_value.reshape(devices, capacity), both, split_axis=0, concat_axis=0, tiled=True
+        partial_value, both, split_axis=0, concat_axis=0, tiled=True
     )
     returned = jnp.sum(returned.reshape(dp_count, expert_count * capacity), axis=0)
     route_value = jnp.stack(
@@ -141,14 +157,19 @@
     weight_table = jnp.broadcast_to(weight_table, (dp_count, experts, capacity))
     row_weight = lax.all_to_all(
         weight_table.reshape(devices, capacity), both, split_axis=0, concat_axis=0, tiled=True
-    ).reshape(-1)
-    spread = jnp.sum(row_weight[:, None] * hidden.astype(jnp.float32), axis=0)
+    )
+    spread, gate_deltas, up_deltas = 0.0, [], []
+    for c, (gate_value, up_value, gate_sig, hidden) in enumerate(kept):
+        weights = row_weight[:, c * chunk : (c + 1) * chunk].reshape(-1)
+        spread = spread + jnp.sum(weights[:, None] * hidden.astype(jnp.float32), axis=0)
+        hidden_grad = weights[:, None] * value_along[None, :]
+        gate_deltas.append(
+            (hidden_grad * up_value * gate_sig * (1.0 + gate_value * (1.0 - gate_sig))).astype(
+                jnp.bfloat16
+            )
+        )
+        up_deltas.append((hidden_grad * gate_value * gate_sig).astype(jnp.bfloat16))
     down_grad = (spread[:, None] * value_weight[None, :]).astype(jnp.bfloat16)
-    hidden_grad = row_weight[:, None] * value_along[None, :]
-    gate_delta = (hidden_grad * up_value * gate_sig * (1.0 + gate_value * (1.0 - gate_sig))).astype(
-        jnp.bfloat16
-    )
-    up_delta = (hidden_grad * gate_value * gate_sig).astype(jnp.bfloat16)
     sigma_grad = (
         prob_grad - jnp.sum(prob_grad * route_prob, axis=1, keepdims=True)
     ) / sigmoid_total
@@ -163,14 +184,15 @@
     )
     parts = jnp.transpose(parts.reshape(experts + 2, devices, -1), (1, 0, 2))
     parts = lax.all_to_all(parts, both, split_axis=0, concat_axis=0, tiled=True)
-    totals = lax.all_gather(jnp.sum(parts, axis=0), both, axis=0, tiled=False)
+    totals = to_all(jnp.sum(parts, axis=0), both)
     totals = jnp.transpose(totals, (1, 0, 2)).reshape(experts + 2, model_width)
-    gate_grad = lax.dot_general(
-        gate_delta, expert_rows, first_first, preferred_element_type=jnp.float32
-    ).astype(jnp.bfloat16)
-    up_grad = lax.dot_general(
-        up_delta, expert_rows, first_first, preferred_element_type=jnp.float32
-    ).astype(jnp.bfloat16)
+    gate_grad, up_grad = [
+        sum(
+            lax.dot_general(delta, rows, first_first, preferred_element_type=jnp.float32)
+            for delta, rows in zip(deltas, row_chunks)
+        ).astype(jnp.bfloat16)
+        for deltas in (gate_deltas, up_deltas)
+    ]
     return (
         own_values[None],
         totals[experts + 1, 0] / divisor,

time: 332 us -> 263 us (0.79)
  blocking collectives: 215 us -> 62.3 us
  waiting for transfers between devices: 6.96 us -> 43.5 us
  matrix products: 59.4 us -> 88.8 us
  starting transfers between devices: 10.3 us -> 24.7 us
    all_gather x2 -> x0, blocking collectives: 137 us -> none  [the longest x1 70.1 us: shards(): totals = lax.all_gather(jnp.sum(parts, axis=0), both, axis=0, tiled=False)]
    dot_general x4 -> x12, matrix products: 41.9 us -> 71.4 us  [the longest x6 44.1 us: shards(): lax.dot_general(delta, rows, first_first, preferred_element_type=jnp.floa...]
    all_to_all x1 -> x4, waiting for transfers between devices: 4.52 us -> 27 us  [the longest x1 18 us: expert_block(): lax.all_to_all(outgoing, 'expert', split_axis=0, concat_axis=0, tiled=True)]
    all_to_all x1 -> x2, blocking collectives: 77.9 us -> 62.3 us  [expert_block(): lax.all_to_all(outgoing, 'expert', split_axis=0, concat_axis=0, tiled=True)]
    all_to_all x1 -> x4, starting transfers between devices: 4.27 us -> 18.1 us  [the longest x2 9.03 us: to_all(): return lax.all_to_all(copies, axes, split_axis=0, concat_axis=0, tiled=True)]
    all_gather x1 -> x3, waiting for transfers between devices: 0.01 us -> 13.6 us  [expert_block(): return lax.all_gather(incoming[None], 'dp', axis=0, tiled=True)]
  transfers between devices with their start and end apart: 4 -> 9, of which waited for: 2 -> 6; matrix products, arithmetic and copies ran while one was open for 10% -> 24% of each run, Pallas kernels for 0% -> 0%
where the time goes in v3:
time: 263 us; the launch traced here: 262 us
  matrix products  88.8 us (34%)
  blocking collectives  62.3 us (24%)
  waiting for transfers between devices  43.5 us (17%)
  starting transfers between devices  24.7 us (9%)
  between operations  18.8 us (7%)
  other arithmetic  12.1 us (5%)
  local copies, waits for them, and re-layouts  12 us (5%)
    all_to_all x2, blocking collectives, expert_block(): lax.all_to_all(outgoing, 'expert', split_axis=0, concat_axis=0, tiled=True)  62.3 us
    dot_general x6, matrix products, shards(): lax.dot_general(delta, rows, first_first, preferred_element_type=jnp.floa...  44.1 us
    all_to_all x1, waiting for transfers between devices, expert_block(): lax.all_to_all(outgoing, 'expert', split_axis=0, concat_axis=0, tiled=True)  18 us
    dot_general x3, matrix products, shards(): lax.dot_general(rows, up_weight[0], last_last, preferred_element_type=jnp...  15.1 us
    all_gather x3, waiting for transfers between devices, expert_block(): return lax.all_gather(incoming[None], 'dp', axis=0, tiled=True)  13.6 us
    dot_general x3, matrix products, shards(): lax.dot_general(rows, gate_weight[0], last_last, preferred_element_type=j...  12.1 us
    all_to_all x2, starting transfers between devices, to_all(): return lax.all_to_all(copies, axes, split_axis=0, concat_axis=0, tiled=True)  9.03 us
    all_to_all x1, waiting for transfers between devices, shards(): lax.all_to_all(partial_value, both, split_axis=0, concat_axis=0, tiled=True)  6.79 us
  transfers between devices with their start and end apart: 9, of which 6 were waited for; matrix products, arithmetic and copies ran while one was open for 24% of the time, Pallas kernels for 0%

profile of v3, /device:TPU:0, one launch (start us, length us, event | category | flops | bytes accessed | tf_op | source)
XLA Modules:
  0.0 262.1 jit_solution(3764933131746517331)
XLA Ops:
  7.2 0.9 copy.40
  8.8 1.5 fusion.18
  10.4 2.3 convolution_convert_fusion
  12.7 1.7 fusion.98
  14.4 33.1 %all_to_all.51 = bf16[8,16,4096]{2,1,0:T(8,128)(2,1)} all-to-all(bf16[8,16,4096]{2,1,0:T(8,128)(2,1)S(1)} %get-tuple-element.48), channel_id=1, replica_groups=mesh['dp'=4,'expert'=8] {'expert'}, dimensions={0} | all-to-all | bytes 2097152 | tf_op jit(solution)/shard_map/all_to_all | solution.py:49
  47.5 29.2 %all_to_all.52 = bf16[8,16,4096]{2,1,0:T(8,128)(2,1)} all-to-all(bf16[8,16,4096]{2,1,0:T(8,128)(2,1)} %get-tuple-element.46), channel_id=1, replica_groups=mesh['dp'=4,'expert'=8] {'expert'}, dimensions={0} | all-to-all | bytes 2097152 | tf_op jit(solution)/shard_map/all_to_all | solution.py:49
  76.7 4.2 %all-to-all-start.2 = ((bf16[8,16,4096]{2,1,0:T(8,128)(2,1)}), bf16[8,16,4096]{2,1,0:T(8,128)(2,1)}, u32[]{:S(2)}, u32[]{:S(2)}) async-start(bf16[8,16,4096]{2,1,0:T(8,128)(2,1)} %get-tuple-element.47), calls=%async_computation.2 | async-start | bytes 2097152 | tf_op jit(solution)/shard_map/all_to_all | solution.py:49
  81.3 2.2 fusion.96
  83.5 4.4 %fusion.21 = f32[384]{0:T(512)S(1)} fusion(f32[4096,1]{0,1:T(1,128)S(1)} %bitcast.140, bf16[1,384,4096]{2,1,0:T(8,128)(2,1)} %param.18), kind=kOutput, calls=%fused_computation.33 | convolution fusion | flops 18874368 | bytes 3163648 | tf_op jit(solution)/shard_map/dot_general | solution.py:124
  87.9 18.0 %all-to-all-done.2 = bf16[8,16,4096]{2,1,0:T(8,128)(2,1)} async-done(((bf16[8,16,4096]{2,1,0:T(8,128)(2,1)}), bf16[8,16,4096]{2,1,0:T(8,128)(2,1)}, u32[]{:S(2)}, u32[]{:S(2)}) %all-to-all-start.2) | async-done | bytes 1048608 | tf_op jit(solution)/shard_map/all_to_all | solution.py:49
  105.9 0.6 broadcast_in_dim.150
  106.5 3.5 %all-to-all-start.4 = ((f32[32,4,128]{2,1,0:T(4,128)}), f32[32,4,128]{2,1,0:T(4,128)S(1)}, u32[]{:S(2)}, u32[]{:S(2)}) async-start(f32[32,4,128]{2,1,0:T(4,128)} %broadcast_in_dim.150), calls=%async_computation.4 | async-start | bytes 131072 | tf_op jit(solution)/shard_map/all_to_all | solution.py:45
  110.7 2.5 fusion.94
  113.3 2.3 copy.46
  115.6 1.7 all-to-all-done.4
  117.3 0.8 slice_reduce_fusion.5
  120.2 0.6 multiply_reduce_fusion
  122.8 5.6 %fusion.8 = f32[512,384]{1,0:T(8,128)} fusion(bf16[512,4096]{1,0:T(8,128)(2,1)} %bitcast.118, bf16[1,384,4096]{2,1,0:T(8,128)(2,1)S(1)} %copy-done), kind=kOutput, calls=%fused_computation.12 | convolution fusion | flops 1610612736 | bytes 8126464 | tf_op jit(solution)/shard_map/dot_general | solution.py:132
  128.4 3.2 %fusion.14 = f32[512,384]{1,0:T(8,128)} fusion(bf16[512,4096]{1,0:T(8,128)(2,1)S(1)} %bitcast.120, bf16[1,384,4096]{2,1,0:T(8,128)(2,1)S(1)} %copy-done.23), kind=kOutput, calls=%fused_computation.18 | convolution fusion | flops 1610612736 | bytes 8126464 | tf_op jit(solution)/shard_map/dot_general | solution.py:129
  131.6 5.6 %fusion.10 = f32[512,384]{1,0:T(8,128)} fusion(bf16[512,4096]{1,0:T(8,128)(2,1)} %bitcast.126, bf16[1,384,4096]{2,1,0:T(8,128)(2,1)S(1)} %copy-done), kind=kOutput, calls=%fused_computation.14 | convolution fusion | flops 1610612736 | bytes 8126464 | tf_op jit(solution)/shard_map/dot_general | solution.py:132
  137.2 3.3 %fusion.16 = f32[512,384]{1,0:T(8,128)} fusion(bf16[512,4096]{1,0:T(8,128)(2,1)S(1)} %bitcast.128, bf16[1,384,4096]{2,1,0:T(8,128)(2,1)S(1)} %copy-done.24), kind=kOutput, calls=%fused_computation.20 | convolution fusion | flops 1610612736 | bytes 8126464 | tf_op jit(solution)/shard_map/dot_general | solution.py:129
  140.4 13.6 %all-gather.11.cloned.1.call-done = bf16[32,16,4096]{2,1,0:T(8,128)(2,1)} async-done(((bf16[8,16,4096]{2,1,0:T(8,128)(2,1)}), bf16[32,16,4096]{2,1,0:T(8,128)(2,1)}) %all-gather.11.cloned.1.call-update) | async-done | bytes 4194320 | tf_op jit(solution)/shard_map/all_gather | solution.py:50
  154.0 5.6 %fusion.12 = f32[512,384]{1,0:T(8,128)S(1)} fusion(bf16[512,4096]{1,0:T(8,128)(2,1)} %bitcast.122, bf16[1,384,4096]{2,1,0:T(8,128)(2,1)} %param.16), kind=kOutput, calls=%fused_computation.16 | convolution fusion | flops 1610612736 | bytes 8126464 | tf_op jit(solution)/shard_map/dot_general | solution.py:129
  159.7 4.0 %fusion.28 = (f32[512]{0:T(512)S(1)}, f32[512]{0:T(512)S(1)}, f32[512]{0:T(512)S(1)}, bf16[512,384]{1,0:T(8,128)(2,1)}, bf16[512,384]{1,0:T(8,128)(2,1)}, /*index=5*/bf16[512,384]{1,0:T(8,128)(2,1)}, f32[512,384]{1,0:T(8,128)}) fusion(f32[384]{0:T(512)S(1)} %fusion.21, f32[512,384]{1,0:T(8,128)S(1)} %fusion.12, f32[512,384]{1,0:T(8,128)S(1)} %copy-done.13, ...), kind=kOutput, calls=%fused_computation.45 | convolution fusion | flops 1615919616 | bytes 13245952 | tf_op jit(solution)/shard_map/dot_general | solution.py:132
  164.0 0.7 pad_maximum_fusion
  164.7 4.8 %all-to-all-start.3 = ((f32[32,1,48]{2,1,0:T(1,128)}), f32[32,1,48]{2,1,0:T(1,128)S(1)}, u32[]{:S(2)}, u32[]{:S(2)}) async-start(f32[32,1,48]{2,1,0:T(1,128)} %bitcast.13), calls=%async_computation.3 | async-start | bytes 32768 | tf_op jit(solution)/shard_map/all_to_all | solution.py:141
  169.5 6.8 %all-to-all-done.3 = f32[32,1,48]{2,1,0:T(1,128)S(1)} async-done(((f32[32,1,48]{2,1,0:T(1,128)}), f32[32,1,48]{2,1,0:T(1,128)S(1)}, u32[]{:S(2)}, u32[]{:S(2)}) %all-to-all-start.3) | async-done | bytes 6176 | tf_op jit(solution)/shard_map/all_to_all | solution.py:141
  176.8 0.7 reduce.26
  177.8 3.3 %multiply_reduce_fusion.3 = (f32[]{:T(128)}, f32[128]{0:T(128)S(1)}, f32[128]{0:T(128)}) fusion(f32[32,128]{1,0:T(8,128)S(1)} %reshape.245, s32[]{:T(128)S(6)} %select_n.39, s32[1,128]{1,0:T(1,128)S(1)} %copy-done.21, f32[128]{0:T(128)S(1)} %get-tuple-element.41, f32[4096,1]{0,1:T(1,128)S(1)} %bitcast.141, bf16[1,128,4096]{2,1,0:T(8,128)(2,1)} %param.12), kind=kOutput, calls=%fused_computation.162 | convolution fusion | flops 6292223 | bytes 1067528 | tf_op jit(solution)/shard_map/dot_general | solution.py:125
  181.4 0.6 broadcast_in_dim.156
  182.0 2.5 all-to-all-start.5
  184.6 2.1 fusion.83
  186.7 1.8 fusion.25
  189.2 2.4 all-to-all-done.5
  191.8 7.0 %fusion.57 = f32[384,4096]{1,0:T(8,128)} fusion(bf16[512,4096]{1,0:T(8,128)(2,1)} %bitcast.127, f32[512,384]{1,0:T(8,128)S(1)} %copy-done.15, f32[512,384]{1,0:T(8,128)S(1)} %copy-done.12, f32[512]{0:T(512)S(1)} %mul.372, f32[384]{0:T(512)S(1)} %fusion.21), kind=kOutput, calls=%fused_computation.75 | convolution fusion | flops 1612775424 | bytes 12062208 | tf_op jit(solution)/shard_map/dot_general | solution.py:191
  198.8 4.7 %fusion.52 = f32[384,4096]{1,0:T(8,128)} fusion(bf16[512,4096]{1,0:T(8,128)(2,1)S(1)} %bitcast.129, f32[512,384]{1,0:T(8,128)S(1)} %copy-done.12, f32[512]{0:T(512)S(1)} %mul.372, f32[384]{0:T(512)S(1)} %fusion.21), kind=kOutput, calls=%fused_computation.73 | convolution fusion | flops 1611988992 | bytes 11275776 | tf_op jit(solution)/shard_map/dot_general | solution.py:191
  203.9 7.4 %fusion.55 = f32[384,4096]{1,0:T(8,128)} fusion(bf16[512,4096]{1,0:T(8,128)(2,1)} %bitcast.119, f32[512,384]{1,0:T(8,128)} %fusion.8, f32[512,384]{1,0:T(8,128)} %fusion.14, f32[512]{0:T(512)S(1)} %mul.375, f32[384]{0:T(512)S(1)} %fusion.21), kind=kOutput, calls=%fused_computation.74 | convolution fusion | flops 1612775424 | bytes 12062208 | tf_op jit(solution)/shard_map/dot_general | solution.py:191
  211.7 2.3 multiply_convert_fusion
  214.0 1.3 fusion.2
  215.3 0.8 maximum_bitcast_fusion
  216.1 3.7 %all-to-all-start.6 = ((f32[32,10,128]{2,1,0:T(8,128)}), f32[32,10,128]{2,1,0:T(8,128)S(1)}, u32[]{:S(2)}, u32[]{:S(2)}) async-start(f32[32,10,128]{2,1,0:T(8,128)} %maximum_bitcast_fusion), calls=%async_computation.6 | async-start | bytes 524288 | tf_op jit(solution)/shard_map/all_to_all | solution.py:186
  219.8 10.2 %fusion = bf16[1,384,4096]{2,1,0:T(8,128)(2,1)} fusion(bf16[512,4096]{1,0:T(8,128)(2,1)} %bitcast.123, f32[384,4096]{1,0:T(8,128)} %fusion.57, f32[384,4096]{1,0:T(8,128)} %fusion.55, f32[512,384]{1,0:T(8,128)} %get-tuple-element.56, f32[512,384]{1,0:T(8,128)} %copy-done.8, f32[512]{0:T(512)S(1)} %mul.378, f32[384]{0:T(512)S(1)} %fusion.21), kind=kOutput, calls=%fused_computation.4 | convolution fusion | flops 1617494016 | bytes 21499392 | tf_op jit(solution)/shard_map/dot_general | solution.py:191
  230.1 4.6 %fusion.50 = f32[384,4096]{1,0:T(8,128)} fusion(bf16[512,4096]{1,0:T(8,128)(2,1)S(1)} %bitcast.121, f32[512,384]{1,0:T(8,128)S(1)} %copy-done.10, f32[512]{0:T(512)S(1)} %mul.375, f32[384]{0:T(512)S(1)} %fusion.21), kind=kOutput, calls=%fused_computation.72 | convolution fusion | flops 1611988992 | bytes 11275776 | tf_op jit(solution)/shard_map/dot_general | solution.py:191
  234.7 0.7 broadcast_in_dim.158
  235.5 5.6 %all-to-all-start.7 = ((f32[32,10,128]{2,1,0:T(8,128)}), f32[32,10,128]{2,1,0:T(8,128)S(1)}, u32[]{:S(2)}, u32[]{:S(2)}) async-start(f32[32,10,128]{2,1,0:T(8,128)} %broadcast_in_dim.158), calls=%async_computation.7 | async-start | bytes 524288 | tf_op jit(solution)/shard_map/all_to_all | solution.py:45
  241.1 10.1 %fusion.1 = bf16[1,384,4096]{2,1,0:T(8,128)(2,1)} fusion(bf16[512,4096]{1,0:T(8,128)(2,1)} %bitcast.124, f32[384,4096]{1,0:T(8,128)} %fusion.52, f32[384,4096]{1,0:T(8,128)} %fusion.50, f32[512,384]{1,0:T(8,128)} %copy-done.8, f32[512]{0:T(512)S(1)} %mul.378, f32[384]{0:T(512)S(1)} %fusion.21), kind=kOutput, calls=%fused_computation.5 | convolution fusion | flops 1616707584 | bytes 20712960 | tf_op jit(solution)/shard_map/dot_general | solution.py:191
  251.8 0.6 slice.170
  252.4 0.7 slice_bitcast_fusion
  (148 shorter events, 7.4 us)
Async XLA Ops:
  7.2 115.6 %copy-start = (bf16[1,384,4096]{2,1,0:T(8,128)(2,1)S(1)}, bf16[1,384,4096]{2,1,0:T(8,128)(2,1)}, u32[]{:S(2)}) copy-start(bf16[1,384,4096]{2,1,0:T(8,128)(2,1)} %param.17) | copy-start | bytes 9437188
  7.2 115.6 %all-gather.9.cloned.1.call-start = ((), (), s32[]{:S(2)}) async-start(), calls=%async_computation.9 | async-start | bytes 5242880 | tf_op jit(solution)/shard_map/all_gather | solution.py:50
  14.3 66.7 %copy-start.21 = (s32[1,128]{1,0:T(1,128)S(1)}, s32[1,128]{1,0:T(1,128)}, u32[]{:S(2)}) copy-start(s32[1,128]{1,0:T(1,128)} %param.21) | copy-start | bytes 1540
  14.3 66.7 %copy-start.27 = (s32[1,128]{1,0:T(1,128)S(1)}, s32[1,128]{1,0:T(1,128)}, u32[]{:S(2)}) copy-start(s32[1,128]{1,0:T(1,128)} %param.20) | copy-start | bytes 1540
  14.3 66.8 %copy-start.26 = (f32[1,8]{1,0:T(1,128)S(1)}, f32[1,8]{1,0:T(1,128)}, u32[]{:S(2)}) copy-start(f32[1,8]{1,0:T(1,128)} %param.23) | copy-start | bytes 100
  14.3 66.9 %copy-start.22 = (f32[1,128]{1,0:T(1,128)S(1)}, f32[1,128]{1,0:T(1,128)}, u32[]{:S(2)}) copy-start(f32[1,128]{1,0:T(1,128)} %param.22) | copy-start | bytes 1540
  14.3 66.9 %copy-start.20 = (f32[4096]{0:T(1024)S(1)}, f32[4096]{0:T(1024)}, u32[]{:S(2)}) copy-start(f32[4096]{0:T(1024)} %param.13) | copy-start | bytes 49156
  14.4 66.9 %copy-start.25 = (f32[8,4096]{1,0:T(8,128)S(1)}, f32[8,4096]{1,0:T(8,128)}, u32[]{:S(2)}) copy-start(f32[8,4096]{1,0:T(8,128)} %param.14) | copy-start | bytes 393220
  47.5 36.0 %copy-start.19 = (f32[4096]{0:T(1024)S(1)}, f32[4096]{0:T(1024)}, u32[]{:S(2)}) copy-start(f32[4096]{0:T(1024)} %param.15) | copy-start | bytes 49156
  47.5 84.1 %all-gather.7.cloned.1.call-start = ((), (), s32[]{:S(2)}) async-start(), calls=%async_computation.8 | async-start | bytes 5242880 | tf_op jit(solution)/shard_map/all_gather | solution.py:50
  76.7 29.1 %all-to-all-start.2 = ((bf16[8,16,4096]{2,1,0:T(8,128)(2,1)}), bf16[8,16,4096]{2,1,0:T(8,128)(2,1)}, u32[]{:S(2)}, u32[]{:S(2)}) async-start(bf16[8,16,4096]{2,1,0:T(8,128)(2,1)} %get-tuple-element.47), calls=%async_computation.2 | async-start | bytes 2097152 | tf_op jit(solution)/shard_map/all_to_all | solution.py:49
  106.5 10.7 %all-to-all-start.4 = ((f32[32,4,128]{2,1,0:T(4,128)}), f32[32,4,128]{2,1,0:T(4,128)S(1)}, u32[]{:S(2)}, u32[]{:S(2)}) async-start(f32[32,4,128]{2,1,0:T(4,128)} %broadcast_in_dim.150), calls=%async_computation.4 | async-start | bytes 131072 | tf_op jit(solution)/shard_map/all_to_all | solution.py:45
  110.0 44.0 %all-gather.11.cloned.1.call-start = ((), (), s32[]{:S(2)}) async-start(), calls=%async_computation.10 | async-start | bytes 5242880 | tf_op jit(solution)/shard_map/all_gather | solution.py:50
  122.8 5.6 %copy-start.2 = (bf16[32,16,4096]{2,1,0:T(8,128)(2,1)S(1)}, bf16[32,16,4096]{2,1,0:T(8,128)(2,1)}, u32[]{:S(2)}) copy-start(bf16[32,16,4096]{2,1,0:T(8,128)(2,1)} %all-gather.9.cloned.1.call-done) | copy-start | bytes 12582916
  122.8 5.6 %copy-start.23 = (bf16[1,384,4096]{2,1,0:T(8,128)(2,1)S(1)}, bf16[1,384,4096]{2,1,0:T(8,128)(2,1)}, u32[]{:S(2)}) copy-start(bf16[1,384,4096]{2,1,0:T(8,128)(2,1)} %param.16) | copy-start | bytes 9437188
  131.6 5.6 %copy-start.5 = (bf16[32,16,4096]{2,1,0:T(8,128)(2,1)S(1)}, bf16[32,16,4096]{2,1,0:T(8,128)(2,1)}, u32[]{:S(2)}) copy-start(bf16[32,16,4096]{2,1,0:T(8,128)(2,1)} %all-gather.7.cloned.1.call-done) | copy-start | bytes 12582916
  131.6 5.6 %copy-start.24 = (bf16[1,384,4096]{2,1,0:T(8,128)(2,1)S(1)}, bf16[1,384,4096]{2,1,0:T(8,128)(2,1)}, u32[]{:S(2)}) copy-start(bf16[1,384,4096]{2,1,0:T(8,128)(2,1)} %param.16) | copy-start | bytes 9437188
  154.0 5.7 %copy-start.4 = (bf16[32,16,4096]{2,1,0:T(8,128)(2,1)S(1)}, bf16[32,16,4096]{2,1,0:T(8,128)(2,1)}, u32[]{:S(2)}) copy-start(bf16[32,16,4096]{2,1,0:T(8,128)(2,1)} %all-gather.11.cloned.1.call-done) | copy-start | bytes 12582916
  154.0 5.7 %copy-start.9 = (f32[512,384]{1,0:T(8,128)S(1)}, f32[512,384]{1,0:T(8,128)}, u32[]{:S(2)}) copy-start(f32[512,384]{1,0:T(8,128)} %fusion.14) | copy-start | bytes 2359300
  154.0 5.7 %copy-start.11 = (f32[512,384]{1,0:T(8,128)S(1)}, f32[512,384]{1,0:T(8,128)}, u32[]{:S(2)}) copy-start(f32[512,384]{1,0:T(8,128)} %fusion.16) | copy-start | bytes 2359300
  154.0 5.7 %copy-start.13 = (f32[512,384]{1,0:T(8,128)S(1)}, f32[512,384]{1,0:T(8,128)}, u32[]{:S(2)}) copy-start(f32[512,384]{1,0:T(8,128)} %fusion.8) | copy-start | bytes 2359300
  154.0 5.7 %copy-start.14 = (f32[512,384]{1,0:T(8,128)S(1)}, f32[512,384]{1,0:T(8,128)}, u32[]{:S(2)}) copy-start(f32[512,384]{1,0:T(8,128)} %fusion.10) | copy-start | bytes 2359300
  159.7 4.0 %copy-start.8 = (f32[512,384]{1,0:T(8,128)}, f32[512,384]{1,0:T(8,128)S(1)}, u32[]{:S(2)}) copy-start(f32[512,384]{1,0:T(8,128)S(1)} %fusion.12) | copy-start | bytes 2359300
  163.7 28.0 %copy-start.12 = (f32[512,384]{1,0:T(8,128)S(1)}, f32[512,384]{1,0:T(8,128)}, u32[]{:S(2)}) copy-start(f32[512,384]{1,0:T(8,128)} %fusion.16) | copy-start | bytes 2359300
  163.7 28.0 %copy-start.15 = (f32[512,384]{1,0:T(8,128)S(1)}, f32[512,384]{1,0:T(8,128)}, u32[]{:S(2)}) copy-start(f32[512,384]{1,0:T(8,128)} %fusion.10) | copy-start | bytes 2359300
  164.7 11.7 %all-to-all-start.3 = ((f32[32,1,48]{2,1,0:T(1,128)}), f32[32,1,48]{2,1,0:T(1,128)S(1)}, u32[]{:S(2)}, u32[]{:S(2)}) async-start(f32[32,1,48]{2,1,0:T(1,128)} %bitcast.13), calls=%async_computation.3 | async-start | bytes 32768 | tf_op jit(solution)/shard_map/all_to_all | solution.py:141
  182.0 9.6 %all-to-all-start.5 = ((f32[32,1,48]{2,1,0:T(1,128)}), f32[32,1,48]{2,1,0:T(1,128)S(1)}, u32[]{:S(2)}, u32[]{:S(2)}) async-start(f32[32,1,48]{2,1,0:T(1,128)} %bitcast.30), calls=%async_computation.5 | async-start | bytes 32768 | tf_op jit(solution)/shard_map/all_to_all | solution.py:158
  191.8 7.0 %copy-start.6 = (bf16[32,16,4096]{2,1,0:T(8,128)(2,1)S(1)}, bf16[32,16,4096]{2,1,0:T(8,128)(2,1)}, u32[]{:S(2)}) copy-start(bf16[32,16,4096]{2,1,0:T(8,128)(2,1)} %all-gather.7.cloned.1.call-done) | copy-start | bytes 12582916
  198.8 4.8 %copy-start.18 = (bf16[512,384]{1,0:T(8,128)(2,1)S(1)}, bf16[512,384]{1,0:T(8,128)(2,1)}, u32[]{:S(2)}) copy-start(bf16[512,384]{1,0:T(8,128)(2,1)} %get-tuple-element.45) | copy-start | bytes 1179652
  203.9 7.5 %copy-start.17 = (bf16[512,384]{1,0:T(8,128)(2,1)S(1)}, bf16[512,384]{1,0:T(8,128)(2,1)}, u32[]{:S(2)}) copy-start(bf16[512,384]{1,0:T(8,128)(2,1)} %get-tuple-element.44) | copy-start | bytes 1179652
  203.9 7.6 %copy-start.16 = (bf16[512,384]{1,0:T(8,128)(2,1)S(1)}, bf16[512,384]{1,0:T(8,128)(2,1)}, u32[]{:S(2)}) copy-start(bf16[512,384]{1,0:T(8,128)(2,1)} %get-tuple-element.43) | copy-start | bytes 1179652
  203.9 10.1 %copy-start.7 = (bf16[1,384,4096]{2,1,0:T(8,128)(2,1)S(1)}, bf16[1,384,4096]{2,1,0:T(8,128)(2,1)}, u32[]{:S(2)}) copy-start(bf16[1,384,4096]{2,1,0:T(8,128)(2,1)} %param.18) | copy-start | bytes 9437188
  216.1 18.6 %all-to-all-start.6 = ((f32[32,10,128]{2,1,0:T(8,128)}), f32[32,10,128]{2,1,0:T(8,128)S(1)}, u32[]{:S(2)}, u32[]{:S(2)}) async-start(f32[32,10,128]{2,1,0:T(8,128)} %maximum_bitcast_fusion), calls=%async_computation.6 | async-start | bytes 524288 | tf_op jit(solution)/shard_map/all_to_all | solution.py:186
  219.8 10.2 %copy-start.3 = (bf16[32,16,4096]{2,1,0:T(8,128)(2,1)S(1)}, bf16[32,16,4096]{2,1,0:T(8,128)(2,1)}, u32[]{:S(2)}) copy-start(bf16[32,16,4096]{2,1,0:T(8,128)(2,1)} %all-gather.9.cloned.1.call-done) | copy-start | bytes 12582916
  219.8 10.2 %copy-start.10 = (f32[512,384]{1,0:T(8,128)S(1)}, f32[512,384]{1,0:T(8,128)}, u32[]{:S(2)}) copy-start(f32[512,384]{1,0:T(8,128)} %fusion.14) | copy-start | bytes 2359300
  235.5 16.2 %all-to-all-start.7 = ((f32[32,10,128]{2,1,0:T(8,128)}), f32[32,10,128]{2,1,0:T(8,128)S(1)}, u32[]{:S(2)}, u32[]{:S(2)}) async-start(f32[32,10,128]{2,1,0:T(8,128)} %broadcast_in_dim.158), calls=%async_computation.7 | async-start | bytes 524288 | tf_op jit(solution)/shard_map/all_to_all | solution.py:45
  241.1 13.3 %copy-start.1 = (bf16[1,384,4096]{2,1,0:T(8,128)(2,1)S(1)}, bf16[1,384,4096]{2,1,0:T(8,128)(2,1)}, u32[]{:S(2)}) copy-start(bf16[1,384,4096]{2,1,0:T(8,128)(2,1)} %param.17) | copy-start | bytes 9437188
Sparse Core Ops, SparseCore 0:
  47.6 33.4 all-gather.8
  82.7 35.1 all-gather.6
  119.4 34.5 all-gather.10

commit v4 on v3

--- a/solution.py
+++ b/solution.py
@@ -45,9 +45,31 @@
     return lax.all_to_all(copies, axes, split_axis=0, concat_axis=0, tiled=True)
 
 
+def across_dp(block):
+    count = lax.axis_size("dp")
+    blocks, bits = {0: block}, count // 2
+    while bits:
+        pairs = [(i, i ^ bits) for i in range(count)]
+        blocks |= {k ^ bits: lax.ppermute(held, "dp", pairs) for k, held in blocks.items()}
+        bits //= 2
+    return jnp.stack([blocks[k] for k in range(count)])
+
+
 def expert_block(outgoing):
     incoming = lax.all_to_all(outgoing, "expert", split_axis=0, concat_axis=0, tiled=True)
-    return lax.all_gather(incoming[None], "dp", axis=0, tiled=True)
+    count = lax.axis_size("dp")
+    if count & (count - 1):
+        return lax.all_gather(incoming, "dp", axis=0)
+    return across_dp(incoming)
+
+
+def reordered(table, count, own):
+    if count & (count - 1):
+        return table
+    turned = jnp.arange(count, dtype=jnp.int32) ^ own
+    hit = turned[:, None] == jnp.arange(count, dtype=jnp.int32)[None, :]
+    hit = hit.reshape(count, count, *(1,) * (table.ndim - 1))
+    return jnp.sum(jnp.where(hit, table[None], 0.0), axis=1)
 
 
 def shards(
@@ -135,9 +157,14 @@
         gate_sig = jax.nn.sigmoid(gate_value)
         hidden = (gate_value * gate_sig * up_value).astype(jnp.bfloat16)
         partial = jnp.sum(hidden.astype(jnp.float32) * value_along[None, :], axis=1)
-        partial_values.append(partial.reshape(devices, chunk))
-        kept.append((gate_value, up_value, gate_sig, hidden))
-    partial_value = jnp.concatenate(partial_values, axis=1)
+        partial_values.append(partial.reshape(dp_count, expert_count, chunk))
+        gate_slope = value_along * up_value * gate_sig * (1.0 + gate_value * (1.0 - gate_sig))
+        up_slope = value_along * gate_value * gate_sig
+        kept.append((rows, hidden, gate_slope, up_slope))
+    expert_rows, hidden, gate_slope, up_slope = [jnp.concatenate(a, axis=0) for a in zip(*kept)]
+    partial_value = reordered(
+        jnp.concatenate(partial_values, axis=2), dp_count, lax.axis_index("dp")
+    ).reshape(devices, capacity)
     returned = lax.all_to_all(
         partial_value, both, split_axis=0, concat_axis=0, tiled=True
     )
@@ -158,17 +185,13 @@
     row_weight = lax.all_to_all(
         weight_table.reshape(devices, capacity), both, split_axis=0, concat_axis=0, tiled=True
     )
-    spread, gate_deltas, up_deltas = 0.0, [], []
-    for c, (gate_value, up_value, gate_sig, hidden) in enumerate(kept):
-        weights = row_weight[:, c * chunk : (c + 1) * chunk].reshape(-1)
-        spread = spread + jnp.sum(weights[:, None] * hidden.astype(jnp.float32), axis=0)
-        hidden_grad = weights[:, None] * value_along[None, :]
-        gate_deltas.append(
-            (hidden_grad * up_value * gate_sig * (1.0 + gate_value * (1.0 - gate_sig))).astype(
-                jnp.bfloat16
-            )
-        )
-        up_deltas.append((hidden_grad * gate_value * gate_sig).astype(jnp.bfloat16))
+    row_weight = reordered(
+        row_weight.reshape(dp_count, expert_count, capacity), dp_count, lax.axis_index("dp")
+    ).reshape(dp_count, expert_count, chunks, chunk)
+    row_weight = jnp.transpose(row_weight, (2, 0, 1, 3)).reshape(-1)
+    spread = jnp.sum(row_weight[:, None] * hidden.astype(jnp.float32), axis=0)
+    gate_delta = (row_weight[:, None] * gate_slope).astype(jnp.bfloat16)
+    up_delta = (row_weight[:, None] * up_slope).astype(jnp.bfloat16)
     down_grad = (spread[:, None] * value_weight[None, :]).astype(jnp.bfloat16)
     sigma_grad = (
         prob_grad - jnp.sum(prob_grad * route_prob, axis=1, keepdims=True)
@@ -187,11 +210,10 @@
     totals = to_all(jnp.sum(parts, axis=0), both)
     totals = jnp.transpose(totals, (1, 0, 2)).reshape(experts + 2, model_width)
     gate_grad, up_grad = [
-        sum(
-            lax.dot_general(delta, rows, first_first, preferred_element_type=jnp.float32)
-            for delta, rows in zip(deltas, row_chunks)
+        lax.dot_general(
+            delta, expert_rows, first_first, preferred_element_type=jnp.float32
         ).astype(jnp.bfloat16)
-        for deltas in (gate_deltas, up_deltas)
+        for delta in (gate_delta, up_delta)
     ]
     return (
         own_values[None],

time: 263 us -> 261 us (level)
  waiting for transfers between devices: 43.5 us -> 95.3 us
  matrix products: 88.8 us -> 55.8 us
  blocking collectives: 62.3 us -> 31.9 us
  starting transfers between devices: 24.7 us -> 37.9 us
  between operations: 18.8 us -> 5.66 us
  other arithmetic: 12.1 us -> 21.1 us
    ppermute x0 -> x9, waiting for transfers between devices: none -> 41.4 us  [across_dp(): lax.ppermute(held, 'dp', pairs)]
    all_to_all x2 -> x1, blocking collectives: 62.3 us -> 31.9 us  [expert_block(): lax.all_to_all(outgoing, 'expert', split_axis=0, concat_axis=0, tiled=True)]
    dot_general x6 -> x2, matrix products: 44.1 us -> 19 us  [shards(): lax.dot_general(delta, expert_rows, first_first, preferred_element_type=j...]
    all_to_all x1 -> x2, waiting for transfers between devices: 18 us -> 35.8 us  [expert_block(): lax.all_to_all(outgoing, 'expert', split_axis=0, concat_axis=0, tiled=True)]
    all_gather x3 -> x0, waiting for transfers between devices: 13.6 us -> none  [expert_block(): return lax.all_gather(incoming[None], 'dp', axis=0, tiled=True)]
    all_to_all x2, waiting for transfers between devices: 2.25 us -> 8.58 us  [to_all(): return lax.all_to_all(copies, axes, split_axis=0, concat_axis=0, tiled=True)]
    another operation x0 -> x3, other arithmetic: none -> 6.06 us  [across_dp(): return jnp.stack([blocks[k] for k in range(count)])]
    dot_general x3, matrix products: 12.1 us -> 7.02 us  [shards(): lax.dot_general(rows, gate_weight[0], last_last, preferred_element_type=j...]
  transfers between devices with their start and end apart: 9 -> 16, of which waited for: 6 -> 9; matrix products, arithmetic and copies ran while one was open for 24% -> 23% of each run, Pallas kernels for 0% -> 0%
where the time goes in v4:
time: 261 us; the launch traced here: 260 us
  waiting for transfers between devices  95.3 us (37%)
  matrix products  55.8 us (21%)
  starting transfers between devices  37.9 us (15%)
  blocking collectives  31.9 us (12%)
  other arithmetic  21.1 us (8%)
  local copies, waits for them, and re-layouts  12.7 us (5%)
  between operations  5.66 us (2%)
    ppermute x9, waiting for transfers between devices, across_dp(): lax.ppermute(held, 'dp', pairs)  41.4 us
    all_to_all x2, waiting for transfers between devices, expert_block(): lax.all_to_all(outgoing, 'expert', split_axis=0, concat_axis=0, tiled=True)  35.8 us
    all_to_all x1, blocking collectives, expert_block(): lax.all_to_all(outgoing, 'expert', split_axis=0, concat_axis=0, tiled=True)  31.9 us
    dot_general x2, matrix products, shards(): lax.dot_general(delta, expert_rows, first_first, preferred_element_type=j...  19 us
    all_to_all x2, starting transfers between devices, to_all(): return lax.all_to_all(copies, axes, split_axis=0, concat_axis=0, tiled=True)  12.9 us
    dot_general x3, matrix products, shards(): lax.dot_general(rows, up_weight[0], last_last, preferred_element_type=jnp...  10.4 us
    all_to_all x2, starting transfers between devices, expert_block(): lax.all_to_all(outgoing, 'expert', split_axis=0, concat_axis=0, tiled=True)  8.66 us
    all_to_all x2, waiting for transfers between devices, to_all(): return lax.all_to_all(copies, axes, split_axis=0, concat_axis=0, tiled=True)  8.58 us
  transfers between devices with their start and end apart: 16, of which 9 were waited for; matrix products, arithmetic and copies ran while one was open for 23% of the time, Pallas kernels for 0%

profile of v4, /device:TPU:0, one launch (start us, length us, event | category | flops | bytes accessed | tf_op | source)
XLA Modules:
  0.0 260.3 jit_solution(17361071794286164314)
XLA Ops:
  0.6 0.8 convert_element_type.86
  1.5 0.8 convert_element_type.84
  4.3 7.3 %all-to-all-start.4 = ((f32[32,4,128]{2,1,0:T(4,128)}), f32[32,4,128]{2,1,0:T(4,128)S(1)}, u32[]{:S(2)}, u32[]{:S(2)}) async-start(f32[32,4,128]{2,1,0:T(4,128)} %broadcast_in_dim.180), calls=%async_computation.4 | async-start | bytes 131072 | tf_op jit(solution)/shard_map/all_to_all | solution.py:45
  11.6 1.5 fusion.20
  13.2 0.8 copy.42
  14.6 2.3 convolution_convert_fusion.2
  16.9 1.8 fusion.53
  18.9 31.9 %all_to_all.48 = bf16[8,16,4096]{2,1,0:T(8,128)(2,1)} all-to-all(bf16[8,16,4096]{2,1,0:T(8,128)(2,1)} %get-tuple-element.47), channel_id=1, replica_groups=mesh['dp'=4,'expert'=8] {'expert'}, dimensions={0} | all-to-all | bytes 2097152 | tf_op jit(solution)/shard_map/all_to_all | solution.py:59
  50.8 4.2 %all-to-all-start.1 = ((bf16[8,16,4096]{2,1,0:T(8,128)(2,1)}), bf16[8,16,4096]{2,1,0:T(8,128)(2,1)}, u32[]{:S(2)}, u32[]{:S(2)}) async-start(bf16[8,16,4096]{2,1,0:T(8,128)(2,1)} %get-tuple-element.48), calls=%async_computation.1 | async-start | bytes 2097152 | tf_op jit(solution)/shard_map/all_to_all | solution.py:59
  55.2 2.3 fusion.51
  57.5 4.5 %fusion.27 = f32[384]{0:T(512)S(1)} fusion(f32[4096,1]{0,1:T(1,128)S(1)} %bitcast.154, bf16[1,384,4096]{2,1,0:T(8,128)(2,1)} %param.18), kind=kOutput, calls=%fused_computation.38 | convolution fusion | flops 18874368 | bytes 3163648 | tf_op jit(solution)/shard_map/dot_general | solution.py:146
  62.0 1.3 fusion.49
  63.2 16.9 %all-to-all-done.1 = bf16[8,16,4096]{2,1,0:T(8,128)(2,1)} async-done(((bf16[8,16,4096]{2,1,0:T(8,128)(2,1)}), bf16[8,16,4096]{2,1,0:T(8,128)(2,1)}, u32[]{:S(2)}, u32[]{:S(2)}) %all-to-all-start.1) | async-done | bytes 1048608 | tf_op jit(solution)/shard_map/all_to_all | solution.py:59
  80.1 4.4 %all-to-all-start = ((bf16[8,16,4096]{2,1,0:T(8,128)(2,1)}), bf16[8,16,4096]{2,1,0:T(8,128)(2,1)}, u32[]{:S(2)}, u32[]{:S(2)}) async-start(bf16[8,16,4096]{2,1,0:T(8,128)(2,1)} %get-tuple-element.46), calls=%async_computation | async-start | bytes 2097152 | tf_op jit(solution)/shard_map/all_to_all | solution.py:59
  84.6 2.3 copy.49
  86.9 0.8 slice_reduce_fusion.5
  87.9 1.5 collective-permute-start.4
  90.8 19.0 %all-to-all-done = bf16[8,16,4096]{2,1,0:T(8,128)(2,1)} async-done(((bf16[8,16,4096]{2,1,0:T(8,128)(2,1)}), bf16[8,16,4096]{2,1,0:T(8,128)(2,1)}, u32[]{:S(2)}, u32[]{:S(2)}) %all-to-all-start) | async-done | bytes 1048608 | tf_op jit(solution)/shard_map/all_to_all | solution.py:59
  109.8 1.5 collective-permute-start.1
  111.3 3.1 %collective-permute-done.4 = bf16[8,16,4096]{2,1,0:T(8,128)(2,1)} collective-permute-done((bf16[8,16,4096]{2,1,0:T(8,128)(2,1)}, bf16[8,16,4096]{2,1,0:T(8,128)(2,1)}, u32[]{:S(2)}, u32[]{:S(2)}) %collective-permute-start.4) | collective-permute-done | bytes 1048608 | tf_op jit(solution)/shard_map/ppermute | solution.py:53
  118.6 18.2 %collective-permute-done.7 = bf16[8,16,4096]{2,1,0:T(8,128)(2,1)} collective-permute-done((bf16[8,16,4096]{2,1,0:T(8,128)(2,1)}, bf16[8,16,4096]{2,1,0:T(8,128)(2,1)}, u32[]{:S(2)}, u32[]{:S(2)}) %collective-permute-start.7) | collective-permute-done | bytes 1048608 | tf_op jit(solution)/shard_map/ppermute | solution.py:53
  136.8 20.1 %collective-permute-done.1 = bf16[8,16,4096]{2,1,0:T(8,128)(2,1)} collective-permute-done((bf16[8,16,4096]{2,1,0:T(8,128)(2,1)}, bf16[8,16,4096]{2,1,0:T(8,128)(2,1)}, u32[]{:S(2)}, u32[]{:S(2)}) %collective-permute-start.1) | collective-permute-done | bytes 1048608 | tf_op jit(solution)/shard_map/ppermute | solution.py:53
  157.0 2.4 pad_maximum_fusion.4
  159.5 2.4 fusion.8
  161.9 1.0 copy-done.11
  162.9 2.3 fusion.14
  165.2 1.8 pad_maximum_fusion.3
  167.0 2.4 fusion.10
  169.4 2.3 fusion.16
  171.8 1.8 pad_maximum_fusion.5
  173.7 2.3 fusion.12
  176.0 5.6 %multiply_reduce_fusion.3 = (f32[512]{0:T(512)S(1)}, f32[512]{0:T(512)S(1)}, f32[512]{0:T(512)S(1)}, bf16[512,384]{1,0:T(8,128)(2,1)}, bf16[512,384]{1,0:T(8,128...) fusion(f32[384]{0:T(512)S(1)} %fusion.27, ...), kind=kOutput, calls=%fused_computation.56 | convolution fusion | flops 1620638208 | bytes 17178112 | tf_op jit(solution)/shard_map/dot_general | solution.py:154
  182.7 5.8 %all-to-all-start.3 = ((f32[32,1,48]{2,1,0:T(1,128)}), f32[32,1,48]{2,1,0:T(1,128)S(1)}, u32[]{:S(2)}, u32[]{:S(2)}) async-start(f32[32,1,48]{2,1,0:T(1,128)} %bitcast.25), calls=%async_computation.3 | async-start | bytes 32768 | tf_op jit(solution)/shard_map/all_to_all | solution.py:168
  188.6 7.0 %all-to-all-done.3 = f32[32,1,48]{2,1,0:T(1,128)S(1)} async-done(((f32[32,1,48]{2,1,0:T(1,128)}), f32[32,1,48]{2,1,0:T(1,128)S(1)}, u32[]{:S(2)}, u32[]{:S(2)}) %all-to-all-start.3) | async-done | bytes 6176 | tf_op jit(solution)/shard_map/all_to_all | solution.py:168
  197.1 3.3 %multiply_reduce_fusion.7 = (f32[]{:T(128)}, f32[128]{0:T(128)S(1)}, f32[128]{0:T(128)}) fusion(f32[32,128]{1,0:T(8,128)S(1)} %reshape.268, s32[]{:T(128)S(6)} %select_n.47, s32[1,128]{1,0:T(1,128)S(1)} %copy-done.10, f32[128]{0:T(128)S(1)} %get-tuple-element.41, f32[4096,1]{0,1:T(1,128)S(1)} %bitcast.155, bf16[1,128,4096]{2,1,0:T(8,128)(2,1)} %param.12), kind=kOutput, calls=%fused_computation.129 | convolution fusion | flops 6292223 | bytes 1067528 | tf_op jit(solution)/shard_map/dot_general | solution.py:147
  201.3 2.5 all-to-all-start.5
  203.9 2.1 fusion.40
  206.0 1.8 fusion.31
  208.5 2.4 all-to-all-done.5
  211.2 1.6 multiply_reduce_fusion
  212.8 3.2 %fusion.2 = f32[1,4096]{1,0:T(1,128)S(1)} fusion(f32[384,1]{0,1:T(1,128)S(1)} %reshape.278, bf16[1,384,4096]{2,1,0:T(8,128)(2,1)} %param.18), kind=kOutput, calls=%fused_computation.10 | convolution fusion | flops 18874368 | bytes 3163648 | tf_op jit(solution)/shard_map/dot_general | solution.py:202
  216.0 0.8 maximum_bitcast_fusion
  216.8 3.7 %all-to-all-start.6 = ((f32[32,10,128]{2,1,0:T(8,128)}), f32[32,10,128]{2,1,0:T(8,128)S(1)}, u32[]{:S(2)}, u32[]{:S(2)}) async-start(f32[32,10,128]{2,1,0:T(8,128)} %maximum_bitcast_fusion), calls=%async_computation.6 | async-start | bytes 524288 | tf_op jit(solution)/shard_map/all_to_all | solution.py:209
  220.5 10.3 %fusion = bf16[1,384,4096]{2,1,0:T(8,128)(2,1)} fusion(bf16[512,4096]{1,0:T(8,128)(2,1)} %bitcast.138, bf16[512,4096]{1,0:T(8,128)(2,1)} %bitcast.130, bf16[512,4096]{1,0:T(8,128)(2,1)} %bitcast.134, f32[512,384]{1,0:T(8,128)} %get-tuple-element.51, f32[512,384]{1,0:T(8,128)} %get-tuple-element.50, f32[512,384]{1,0:T(8,128)} %get-tuple-element.49, ...), kind=kOutput, calls=%fused_computation.5 | convolution fusion | flops 4873519104 | bytes 18094080 | tf_op jit(solution)/shard_map/dot_general | solution.py:213
  230.8 8.7 %fusion.1 = bf16[1,384,4096]{2,1,0:T(8,128)(2,1)} fusion(bf16[512,4096]{1,0:T(8,128)(2,1)} %bitcast.139, bf16[512,4096]{1,0:T(8,128)(2,1)S(1)} %bitcast.131, bf16[512,4096]{1,0:T(8,128)(2,1)S(1)} %bitcast.135, f32[512,384]{1,0:T(8,128)} %get-tuple-element.54, f32[512,384]{1,0:T(8,128)} %get-tuple-element.53, f32[512,384]{1,0:T(8,128)S(1)} %copy-done.12, ...), kind=kOutput, calls=%fused_computation.6 | convolution fusion | flops 4873519104 | bytes 18094080 | tf_op jit(solution)/shard_map/dot_general | solution.py:213
  240.3 5.6 %all-to-all-start.7 = ((f32[32,10,128]{2,1,0:T(8,128)}), f32[32,10,128]{2,1,0:T(8,128)S(1)}, u32[]{:S(2)}, u32[]{:S(2)}) async-start(f32[32,10,128]{2,1,0:T(8,128)} %broadcast_in_dim.190), calls=%async_computation.7 | async-start | bytes 524288 | tf_op jit(solution)/shard_map/all_to_all | solution.py:45
  245.8 2.3 multiply_convert_fusion
  248.1 8.3 %all-to-all-done.7 = f32[32,10,128]{2,1,0:T(8,128)S(1)} async-done(((f32[32,10,128]{2,1,0:T(8,128)}), f32[32,10,128]{2,1,0:T(8,128)S(1)}, u32[]{:S(2)}, u32[]{:S(2)}) %all-to-all-start.7) | async-done | bytes 163872 | tf_op jit(solution)/shard_map/all_to_all | solution.py:45
  (127 shorter events, 13.6 us)
Async XLA Ops:
  0.6 158.8 %copy-start = (bf16[1,384,4096]{2,1,0:T(8,128)(2,1)S(1)}, bf16[1,384,4096]{2,1,0:T(8,128)(2,1)}, u32[]{:S(2)}) copy-start(bf16[1,384,4096]{2,1,0:T(8,128)(2,1)} %param.17) | copy-start | bytes 9437188
  4.3 14.6 %all-to-all-start.4 = ((f32[32,4,128]{2,1,0:T(4,128)}), f32[32,4,128]{2,1,0:T(4,128)S(1)}, u32[]{:S(2)}, u32[]{:S(2)}) async-start(f32[32,4,128]{2,1,0:T(4,128)} %broadcast_in_dim.180), calls=%async_computation.4 | async-start | bytes 131072 | tf_op jit(solution)/shard_map/all_to_all | solution.py:45
  18.7 36.5 %copy-start.9 = (f32[4096]{0:T(1024)S(1)}, f32[4096]{0:T(1024)}, u32[]{:S(2)}) copy-start(f32[4096]{0:T(1024)} %param.13) | copy-start | bytes 49156
  18.7 38.8 %copy-start.8 = (f32[4096]{0:T(1024)S(1)}, f32[4096]{0:T(1024)}, u32[]{:S(2)}) copy-start(f32[4096]{0:T(1024)} %param.15) | copy-start | bytes 49156
  50.8 29.3 %all-to-all-start.1 = ((bf16[8,16,4096]{2,1,0:T(8,128)(2,1)}), bf16[8,16,4096]{2,1,0:T(8,128)(2,1)}, u32[]{:S(2)}, u32[]{:S(2)}) async-start(bf16[8,16,4096]{2,1,0:T(8,128)(2,1)} %get-tuple-element.48), calls=%async_computation.1 | async-start | bytes 2097152 | tf_op jit(solution)/shard_map/all_to_all | solution.py:59
  55.1 6.9 %copy-start.1 = (bf16[1,128,4096]{2,1,0:T(8,128)(2,1)S(1)}, bf16[1,128,4096]{2,1,0:T(8,128)(2,1)}, u32[]{:S(2)}) copy-start(bf16[1,128,4096]{2,1,0:T(8,128)(2,1)} %param.12) | copy-start | bytes 3145732
  80.1 29.7 %all-to-all-start = ((bf16[8,16,4096]{2,1,0:T(8,128)(2,1)}), bf16[8,16,4096]{2,1,0:T(8,128)(2,1)}, u32[]{:S(2)}, u32[]{:S(2)}) async-start(bf16[8,16,4096]{2,1,0:T(8,128)(2,1)} %get-tuple-element.46), calls=%async_computation | async-start | bytes 2097152 | tf_op jit(solution)/shard_map/all_to_all | solution.py:59
  87.9 26.4 %collective-permute-start.4 = (bf16[8,16,4096]{2,1,0:T(8,128)(2,1)}, bf16[8,16,4096]{2,1,0:T(8,128)(2,1)}, u32[]{:S(2)}, u32[]{:S(2)}) collective-permute-start(bf16[8,16,4096]{2,1,0:T(8,128)(2,1)} %all-to-all-done.1), channel_id=1, source_target_pairs={{0,16},{8,24},{16,0},{24,8},{1,17},{9,25},{17,1},{25,9},{2,18},{10... | collective-permute-start | bytes 3145736 | tf_op jit(solution)/shard_map/ppermute | solution.py:53
  90.2 28.3 %collective-permute-start.3 = (bf16[8,16,4096]{2,1,0:T(8,128)(2,1)}, bf16[8,16,4096]{2,1,0:T(8,128)(2,1)}, u32[]{:S(2)}, u32[]{:S(2)}) collective-permute-start(bf16[8,16,4096]{2,1,0:T(8,128)(2,1)} %all-to-all-done.1), channel_id=1, source_target_pairs={{0,8},{8,0},{16,24},{24,16},{1,9},{9,1},{17,25},{25,17},{2,10},{10... | collective-permute-start | bytes 3145736 | tf_op jit(solution)/shard_map/ppermute | solution.py:53
  90.2 46.6 %collective-permute-start.7 = (bf16[8,16,4096]{2,1,0:T(8,128)(2,1)}, bf16[8,16,4096]{2,1,0:T(8,128)(2,1)}, u32[]{:S(2)}, u32[]{:S(2)}) collective-permute-start(bf16[8,16,4096]{2,1,0:T(8,128)(2,1)} %all_to_all.48), channel_id=1, source_target_pairs={{0,16},{8,24},{16,0},{24,8},{1,17},{9,25},{17,1},{25,9},{2,18},{10... | collective-permute-start | bytes 3145736 | tf_op jit(solution)/shard_map/ppermute | solution.py:53
  109.8 47.2 %collective-permute-start.1 = (bf16[8,16,4096]{2,1,0:T(8,128)(2,1)}, bf16[8,16,4096]{2,1,0:T(8,128)(2,1)}, u32[]{:S(2)}, u32[]{:S(2)}) collective-permute-start(bf16[8,16,4096]{2,1,0:T(8,128)(2,1)} %all-to-all-done), channel_id=1, source_target_pairs={{0,16},{8,24},{16,0},{24,8},{1,17},{9,25},{17,1},{25,9},{2,18},{10... | collective-permute-start | bytes 3145736 | tf_op jit(solution)/shard_map/ppermute | solution.py:53
  114.4 42.6 %collective-permute-start.5 = (bf16[8,16,4096]{2,1,0:T(8,128)(2,1)}, bf16[8,16,4096]{2,1,0:T(8,128)(2,1)}, u32[]{:S(2)}, u32[]{:S(2)}) collective-permute-start(bf16[8,16,4096]{2,1,0:T(8,128)(2,1)} %collective-permute-done.4), channel_id=1, source_target_pairs={{0,8},{8,0},{16,24},{24,16},{1,9},{9,1},{17,25},{25,17},{2,10},{10... | collective-permute-start | bytes 3145736 | tf_op jit(solution)/shard_map/ppermute | solution.py:53
  118.0 53.8 %collective-permute-start.6 = (bf16[8,16,4096]{2,1,0:T(8,128)(2,1)}, bf16[8,16,4096]{2,1,0:T(8,128)(2,1)S(1)}, u32[]{:S(2)}, u32[]{:S(2)}) collective-permute-start(bf16[8,16,4096]{2,1,0:T(8,128)(2,1)} %all_to_all.48), channel_id=1, source_target_pairs={{0,8},{8,0},{16,24},{24,16},{1,9},{9,1},{17,25},{25,17},{2,10},{10... | collective-permute-start | bytes 3145736 | tf_op jit(solution)/shard_map/ppermute | solution.py:53
  118.5 46.7 %collective-permute-start = (bf16[8,16,4096]{2,1,0:T(8,128)(2,1)}, bf16[8,16,4096]{2,1,0:T(8,128)(2,1)S(1)}, u32[]{:S(2)}, u32[]{:S(2)}) collective-permute-start(bf16[8,16,4096]{2,1,0:T(8,128)(2,1)} %all-to-all-done), channel_id=1, source_target_pairs={{0,8},{8,0},{16,24},{24,16},{1,9},{9,1},{17,25},{25,17},{2,10},{10... | collective-permute-start | bytes 3145736 | tf_op jit(solution)/shard_map/ppermute | solution.py:53
  136.8 35.0 %collective-permute-start.8 = (bf16[8,16,4096]{2,1,0:T(8,128)(2,1)}, bf16[8,16,4096]{2,1,0:T(8,128)(2,1)S(1)}, u32[]{:S(2)}, u32[]{:S(2)}) collective-permute-start(bf16[8,16,4096]{2,1,0:T(8,128)(2,1)} %collective-permute-done.7), channel_id=1, source_target_pairs={{0,8},{8,0},{16,24},{24,16},{1,9},{9,1},{17,25},{25,17},{2,10},{10... | collective-permute-start | bytes 3145736 | tf_op jit(solution)/shard_map/ppermute | solution.py:53
  157.0 8.2 %collective-permute-start.2 = (bf16[8,16,4096]{2,1,0:T(8,128)(2,1)}, bf16[8,16,4096]{2,1,0:T(8,128)(2,1)S(1)}, u32[]{:S(2)}, u32[]{:S(2)}) collective-permute-start(bf16[8,16,4096]{2,1,0:T(8,128)(2,1)} %collective-permute-done.1), channel_id=1, source_target_pairs={{0,8},{8,0},{16,24},{24,16},{1,9},{9,1},{17,25},{25,17},{2,10},{10... | collective-permute-start | bytes 3145736 | tf_op jit(solution)/shard_map/ppermute | solution.py:53
  159.4 2.4 copy-start.2
  159.4 3.4 %copy-start.11 = (bf16[1,384,4096]{2,1,0:T(8,128)(2,1)S(1)}, bf16[1,384,4096]{2,1,0:T(8,128)(2,1)}, u32[]{:S(2)}) copy-start(bf16[1,384,4096]{2,1,0:T(8,128)(2,1)} %param.16) | copy-start | bytes 9437188
  167.0 2.4 copy-start.4
  169.4 2.4 copy-start.7
  173.7 2.4 copy-start.6
  176.0 21.0 %copy-start.10 = (s32[1,128]{1,0:T(1,128)S(1)}, s32[1,128]{1,0:T(1,128)}, u32[]{:S(2)}) copy-start(s32[1,128]{1,0:T(1,128)} %param.21) | copy-start | bytes 1540
  182.7 12.9 %all-to-all-start.3 = ((f32[32,1,48]{2,1,0:T(1,128)}), f32[32,1,48]{2,1,0:T(1,128)S(1)}, u32[]{:S(2)}, u32[]{:S(2)}) async-start(f32[32,1,48]{2,1,0:T(1,128)} %bitcast.25), calls=%async_computation.3 | async-start | bytes 32768 | tf_op jit(solution)/shard_map/all_to_all | solution.py:168
  201.3 9.6 %all-to-all-start.5 = ((f32[32,1,48]{2,1,0:T(1,128)}), f32[32,1,48]{2,1,0:T(1,128)S(1)}, u32[]{:S(2)}, u32[]{:S(2)}) async-start(f32[32,1,48]{2,1,0:T(1,128)} %bitcast.42), calls=%async_computation.5 | async-start | bytes 32768 | tf_op jit(solution)/shard_map/all_to_all | solution.py:185
  216.8 22.7 %all-to-all-start.6 = ((f32[32,10,128]{2,1,0:T(8,128)}), f32[32,10,128]{2,1,0:T(8,128)S(1)}, u32[]{:S(2)}, u32[]{:S(2)}) async-start(f32[32,10,128]{2,1,0:T(8,128)} %maximum_bitcast_fusion), calls=%async_computation.6 | async-start | bytes 524288 | tf_op jit(solution)/shard_map/all_to_all | solution.py:209
  220.5 10.3 %copy-start.3 = (bf16[4,8,16,4096]{3,2,1,0:T(8,128)(2,1)S(1)}, bf16[4,8,16,4096]{3,2,1,0:T(8,128)(2,1)}, u32[]{:S(2)}) copy-start(bf16[4,8,16,4096]{3,2,1,0:T(8,128)(2,1)} %copy-done.2) | copy-start | bytes 12582916
  220.5 10.3 %copy-start.5 = (bf16[4,8,16,4096]{3,2,1,0:T(8,128)(2,1)S(1)}, bf16[4,8,16,4096]{3,2,1,0:T(8,128)(2,1)}, u32[]{:S(2)}) copy-start(bf16[4,8,16,4096]{3,2,1,0:T(8,128)(2,1)} %copy-done.4) | copy-start | bytes 12582916
  220.5 10.3 %copy-start.12 = (f32[512,384]{1,0:T(8,128)S(1)}, f32[512,384]{1,0:T(8,128)}, u32[]{:S(2)}) copy-start(f32[512,384]{1,0:T(8,128)} %get-tuple-element.52) | copy-start | bytes 2359300
  240.3 16.2 %all-to-all-start.7 = ((f32[32,10,128]{2,1,0:T(8,128)}), f32[32,10,128]{2,1,0:T(8,128)S(1)}, u32[]{:S(2)}, u32[]{:S(2)}) async-start(f32[32,10,128]{2,1,0:T(8,128)} %broadcast_in_dim.190), calls=%async_computation.7 | async-start | bytes 524288 | tf_op jit(solution)/shard_map/all_to_all | solution.py:45

commit v5 on v4

--- a/solution.py
+++ b/solution.py
@@ -45,22 +45,35 @@
     return lax.all_to_all(copies, axes, split_axis=0, concat_axis=0, tiled=True)
 
 
-def across_dp(block):
+def across_bit(blocks, bits):
     count = lax.axis_size("dp")
-    blocks, bits = {0: block}, count // 2
-    while bits:
-        pairs = [(i, i ^ bits) for i in range(count)]
-        blocks |= {k ^ bits: lax.ppermute(held, "dp", pairs) for k, held in blocks.items()}
-        bits //= 2
-    return jnp.stack([blocks[k] for k in range(count)])
-
-
-def expert_block(outgoing):
-    incoming = lax.all_to_all(outgoing, "expert", split_axis=0, concat_axis=0, tiled=True)
+    pairs = [(i, i ^ bits) for i in range(count)]
+    return blocks | {k ^ bits: lax.ppermute(held, "dp", pairs) for k, held in blocks.items()}
+
+
+def expert_chunks(outgoing, chunks):
     count = lax.axis_size("dp")
+    chunk = outgoing.shape[1] // chunks
+    parts = [outgoing[:, c * chunk : (c + 1) * chunk] for c in range(chunks)]
+    held = []
+    for c in range(chunks):
+        part = parts[c]
+        if c > 1 and not count & (count - 1):
+            part, held[c - 2] = lax.optimization_barrier((part, held[c - 2]))
+        incoming = lax.all_to_all(part, "expert", split_axis=0, concat_axis=0, tiled=True)
+        if count & (count - 1):
+            held.append(lax.all_gather(incoming, "dp", axis=0))
+        else:
+            held.append(across_bit({0: incoming}, count // 2) if count > 1 else {0: incoming})
     if count & (count - 1):
-        return lax.all_gather(incoming, "dp", axis=0)
-    return across_dp(incoming)
+        return held
+    stacked = []
+    for blocks in held:
+        bits = count // 4
+        while bits:
+            blocks, bits = across_bit(blocks, bits), bits // 2
+        stacked.append(jnp.stack([blocks[k] for k in range(count)]))
+    return stacked
 
 
 def reordered(table, count, own):
@@ -119,10 +132,7 @@
     outgoing = outgoing.reshape(experts, capacity, model_width)
     chunks = max(capacity // 16, 1)
     chunk = capacity // chunks
-    row_chunks = [
-        expert_block(outgoing[:, c * chunk : (c + 1) * chunk]).reshape(-1, model_width)
-        for c in range(chunks)
-    ]
+    row_chunks = [rows.reshape(-1, model_width) for rows in expert_chunks(outgoing, chunks)]
 
     normed_float = normed.astype(jnp.float32)
     logits = lax.dot_general(normed_float, router_weight, last_last, precision=highest)

time: 261 us -> 235 us (0.900)
  blocking collectives: 31.9 us -> 0 us
  starting transfers between devices: 37.9 us -> 45.3 us
  waiting for transfers between devices: 95.3 us -> 88.5 us
  local copies, waits for them, and re-layouts: 12.7 us -> 15.5 us
    all_to_all x1 -> x0, blocking collectives: 31.9 us -> none  [expert_block(): lax.all_to_all(outgoing, 'expert', split_axis=0, concat_axis=0, tiled=True)]
    ppermute x9, waiting for transfers between devices: 41.4 us -> 28.6 us  [across_bit(): lax.ppermute(held, 'dp', pairs)]
    all_to_all x2 -> x3, starting transfers between devices: 8.66 us -> 16.2 us  [expert_chunks(): lax.all_to_all(part, 'expert', split_axis=0, concat_axis=0, tiled=True)]
    all_to_all x2 -> x3, waiting for transfers between devices: 35.8 us -> 41.9 us  [expert_chunks(): lax.all_to_all(part, 'expert', split_axis=0, concat_axis=0, tiled=True)]
    unnamed x29 -> x31, local copies, waits for them, and re-layouts: 2.03 us -> 4.77 us
  transfers between devices with their start and end apart: 16 -> 17, of which waited for: 9 -> 10; matrix products, arithmetic and copies ran while one was open for 23% -> 26% of each run, Pallas kernels for 0% -> 0%
where the time goes in v5:
time: 235 us; the launch traced here: 234 us
  waiting for transfers between devices  88.5 us (38%)
  matrix products  56.7 us (24%)
  starting transfers between devices  45.3 us (19%)
  other arithmetic  22 us (9%)
  local copies, waits for them, and re-layouts  15.5 us (7%)
  between operations  5.62 us (2%)
    all_to_all x3, waiting for transfers between devices, expert_chunks(): lax.all_to_all(part, 'expert', split_axis=0, concat_axis=0, tiled=True)  41.9 us
    ppermute x9, waiting for transfers between devices, across_bit(): lax.ppermute(held, 'dp', pairs)  28.6 us
    dot_general x2, matrix products, shards(): lax.dot_general(delta, expert_rows, first_first, preferred_element_type=j...  19 us
    all_to_all x3, starting transfers between devices, expert_chunks(): lax.all_to_all(part, 'expert', split_axis=0, concat_axis=0, tiled=True)  16.2 us
    all_to_all x2, starting transfers between devices, to_all(): return lax.all_to_all(copies, axes, split_axis=0, concat_axis=0, tiled=True)  12.9 us
    dot_general x3, matrix products, shards(): lax.dot_general(rows, up_weight[0], last_last, preferred_element_type=jnp...  11.3 us
    all_to_all x2, waiting for transfers between devices, to_all(): return lax.all_to_all(copies, axes, split_axis=0, concat_axis=0, tiled=True)  8.57 us
    dot_general x3, matrix products, shards(): lax.dot_general(rows, gate_weight[0], last_last, preferred_element_type=j...  7.03 us
  transfers between devices with their start and end apart: 17, of which 10 were waited for; matrix products, arithmetic and copies ran while one was open for 26% of the time, Pallas kernels for 0%

profile of v5, /device:TPU:0, one launch (start us, length us, event | category | flops | bytes accessed | tf_op | source)
XLA Modules:
  0.0 233.6 jit_solution(8461285473593542489)
XLA Ops:
  0.6 0.8 convert_element_type.86
  4.3 7.3 %all-to-all-start.4 = ((f32[32,4,128]{2,1,0:T(4,128)}), f32[32,4,128]{2,1,0:T(4,128)S(1)}, u32[]{:S(2)}, u32[]{:S(2)}) async-start(f32[32,4,128]{2,1,0:T(4,128)} %broadcast_in_dim.180), calls=%async_computation.4 | async-start | bytes 131072 | tf_op jit(solution)/shard_map/all_to_all | solution.py:45
  11.6 1.5 fusion.20
  14.6 2.3 convolution_convert_fusion.2
  16.9 1.8 fusion.53
  18.9 5.7 %all-to-all-start = ((bf16[8,16,4096]{2,1,0:T(8,128)(2,1)}), bf16[8,16,4096]{2,1,0:T(8,128)(2,1)}, u32[]{:S(2)}, u32[]{:S(2)}) async-start(bf16[8,16,4096]{2,1,0:T(8,128)(2,1)} %get-tuple-element.53), calls=%async_computation | async-start | bytes 2097152 | tf_op jit(solution)/shard_map/all_to_all | solution.py:63
  24.8 2.3 fusion.51
  27.1 4.5 %fusion.27 = f32[384]{0:T(512)S(1)} fusion(f32[4096,1]{0,1:T(1,128)S(1)} %bitcast.152, bf16[1,384,4096]{2,1,0:T(8,128)(2,1)} %param.18), kind=kOutput, calls=%fused_computation.38 | convolution fusion | flops 18874368 | bytes 3163648 | tf_op jit(solution)/shard_map/dot_general | solution.py:156
  31.6 1.4 fusion.49
  32.9 17.9 %all-to-all-done = bf16[8,16,4096]{2,1,0:T(8,128)(2,1)} async-done(((bf16[8,16,4096]{2,1,0:T(8,128)(2,1)}), bf16[8,16,4096]{2,1,0:T(8,128)(2,1)}, u32[]{:S(2)}, u32[]{:S(2)}) %all-to-all-start) | async-done | bytes 1048608 | tf_op jit(solution)/shard_map/all_to_all | solution.py:63
  50.8 4.2 %all-to-all-start.1 = ((bf16[8,16,4096]{2,1,0:T(8,128)(2,1)}), bf16[8,16,4096]{2,1,0:T(8,128)(2,1)}, u32[]{:S(2)}, u32[]{:S(2)}) async-start(bf16[8,16,4096]{2,1,0:T(8,128)(2,1)} %get-tuple-element.52), calls=%async_computation.1 | async-start | bytes 2097152 | tf_op jit(solution)/shard_map/all_to_all | solution.py:63
  55.1 2.3 copy.49
  58.5 1.5 collective-permute-start
  60.7 20.0 %all-to-all-done.1 = bf16[8,16,4096]{2,1,0:T(8,128)(2,1)} async-done(((bf16[8,16,4096]{2,1,0:T(8,128)(2,1)}), bf16[8,16,4096]{2,1,0:T(8,128)(2,1)}, u32[]{:S(2)}, u32[]{:S(2)}) %all-to-all-start.1) | async-done | bytes 1048608 | tf_op jit(solution)/shard_map/all_to_all | solution.py:63
  80.7 1.5 collective-permute-start.4
  82.2 1.9 collective-permute-done
  84.8 6.3 %all-to-all-start.2 = ((bf16[8,16,4096]{2,1,0:T(8,128)(2,1)}), bf16[8,16,4096]{2,1,0:T(8,128)(2,1)}, u32[]{:S(2)}, u32[]{:S(2)}) async-start(bf16[8,16,4096]{2,1,0:T(8,128)(2,1)} %get-tuple-element.12), calls=%async_computation.2 | async-start | bytes 2097152 | tf_op jit(solution)/shard_map/all_to_all | solution.py:63
  94.5 11.0 %collective-permute-done.4 = bf16[8,16,4096]{2,1,0:T(8,128)(2,1)} collective-permute-done((bf16[8,16,4096]{2,1,0:T(8,128)(2,1)}, bf16[8,16,4096]{2,1,0:T(8,128)(2,1)}, u32[]{:S(2)}, u32[]{:S(2)}) %collective-permute-start.4) | collective-permute-done | bytes 1048608 | tf_op jit(solution)/shard_map/ppermute | solution.py:51
  105.5 2.4 %pad_maximum_fusion.3 = bf16[4,8,16,4096]{3,2,1,0:T(8,128)(2,1)S(1)} fusion(bf16[1,8,16,4096]{3,2,1,0:T(8,128)(2,1)} %bitcast.8, bf16[1,8,16,4096]{3,2,1,0:T(8,128)(2,1)} %bitcast.7, bf16[1,8,16,4096]{3,2,1,0:T(8,128)(2,1)} %bitcast.6, bf16[1,8,16,4096]{3,2,1,0:T(8,128)(2,1)} %bitcast.5), kind=kLoop, calls=%fused_computation.7 | loop fusion | flops 6291456 | bytes 8388608 | tf_op jit(solution)/shard_map/stack | solution.py:75
  107.9 1.9 copy-done.2
  109.8 3.3 %fusion.10 = f32[512,384]{1,0:T(8,128)} fusion(bf16[512,4096]{1,0:T(8,128)(2,1)S(1)} %bitcast.128, bf16[1,384,4096]{2,1,0:T(8,128)(2,1)S(1)} %copy-done), kind=kOutput, calls=%fused_computation.18 | convolution fusion | flops 1610612736 | bytes 8126464 | tf_op jit(solution)/shard_map/dot_general | solution.py:164
  113.1 4.0 %all-to-all-done.2 = bf16[8,16,4096]{2,1,0:T(8,128)(2,1)} async-done(((bf16[8,16,4096]{2,1,0:T(8,128)(2,1)}), bf16[8,16,4096]{2,1,0:T(8,128)(2,1)}, u32[]{:S(2)}, u32[]{:S(2)}) %all-to-all-start.2) | async-done | bytes 1048608 | tf_op jit(solution)/shard_map/all_to_all | solution.py:63
  117.1 1.5 collective-permute-start.7
  118.6 2.6 %pad_maximum_fusion.4 = bf16[4,8,16,4096]{3,2,1,0:T(8,128)(2,1)S(1)} fusion(bf16[1,8,16,4096]{3,2,1,0:T(8,128)(2,1)} %bitcast.17, bf16[1,8,16,4096]{3,2,1,0:T(8,128)(2,1)} %bitcast.16, bf16[1,8,16,4096]{3,2,1,0:T(8,128)(2,1)} %bitcast.15, bf16[1,8,16,4096]{3,2,1,0:T(8,128)(2,1)} %bitcast.14), kind=kLoop, calls=%fused_computation.8 | loop fusion | flops 6291456 | bytes 8388608 | tf_op jit(solution)/shard_map/stack | solution.py:75
  121.2 0.8 copy-done.3
  122.1 1.0 copy-done.11
  123.1 2.3 %fusion.16 = f32[512,384]{1,0:T(8,128)S(1)} fusion(bf16[512,4096]{1,0:T(8,128)(2,1)S(1)} %bitcast.130, bf16[1,384,4096]{2,1,0:T(8,128)(2,1)S(1)} %copy-done.11), kind=kOutput, calls=%fused_computation.24 | convolution fusion | flops 1610612736 | bytes 8126464 | tf_op jit(solution)/shard_map/dot_general | solution.py:161
  125.5 15.8 %collective-permute-done.7 = bf16[8,16,4096]{2,1,0:T(8,128)(2,1)S(1)} collective-permute-done((bf16[8,16,4096]{2,1,0:T(8,128)(2,1)}, bf16[8,16,4096]{2,1,0:T(8,128)(2,1)S(1)}, u32[]{:S(2)}, u32[]{:S(2)}) %collective-permute-start.7) | collective-permute-done | bytes 1048608 | tf_op jit(solution)/shard_map/ppermute | solution.py:51
  141.3 2.4 %fusion.8 = f32[512,384]{1,0:T(8,128)S(1)} fusion(bf16[512,4096]{1,0:T(8,128)(2,1)S(1)} %bitcast.132, bf16[1,384,4096]{2,1,0:T(8,128)(2,1)S(1)} %copy-done), kind=kOutput, calls=%fused_computation.16 | convolution fusion | flops 1610612736 | bytes 8126464 | tf_op jit(solution)/shard_map/dot_general | solution.py:164
  143.7 2.3 %fusion.14 = f32[512,384]{1,0:T(8,128)S(1)} fusion(bf16[512,4096]{1,0:T(8,128)(2,1)S(1)} %bitcast.133, bf16[1,384,4096]{2,1,0:T(8,128)(2,1)S(1)} %copy-done.11), kind=kOutput, calls=%fused_computation.22 | convolution fusion | flops 1610612736 | bytes 8126464 | tf_op jit(solution)/shard_map/dot_general | solution.py:161
  146.1 1.8 pad_maximum_fusion.5
  147.9 2.3 %fusion.12 = f32[512,384]{1,0:T(8,128)S(1)} fusion(bf16[512,4096]{1,0:T(8,128)(2,1)S(1)} %bitcast.136, bf16[1,384,4096]{2,1,0:T(8,128)(2,1)S(1)} %copy-done.11), kind=kOutput, calls=%fused_computation.20 | convolution fusion | flops 1610612736 | bytes 8126464 | tf_op jit(solution)/shard_map/dot_general | solution.py:161
  150.3 5.6 %multiply_reduce_fusion.3 = (f32[512]{0:T(512)S(1)}, f32[512]{0:T(512)S(1)}, f32[512]{0:T(512)S(1)}, bf16[512,384]{1,0:T(8,128)(2,1)}, bf16[512,384]{1,0:T(8,128...) fusion(f32[384]{0:T(512)S(1)} %fusion.27, ...), kind=kOutput, calls=%fused_computation.56 | convolution fusion | flops 1620638208 | bytes 17178112 | tf_op jit(solution)/shard_map/dot_general | solution.py:164
  156.9 4.9 %all-to-all-start.3 = ((f32[32,1,48]{2,1,0:T(1,128)}), f32[32,1,48]{2,1,0:T(1,128)S(1)}, u32[]{:S(2)}, u32[]{:S(2)}) async-start(f32[32,1,48]{2,1,0:T(1,128)} %bitcast.25), calls=%async_computation.3 | async-start | bytes 32768 | tf_op jit(solution)/shard_map/all_to_all | solution.py:178
  161.9 7.0 %all-to-all-done.3 = f32[32,1,48]{2,1,0:T(1,128)S(1)} async-done(((f32[32,1,48]{2,1,0:T(1,128)}), f32[32,1,48]{2,1,0:T(1,128)S(1)}, u32[]{:S(2)}, u32[]{:S(2)}) %all-to-all-start.3) | async-done | bytes 6176 | tf_op jit(solution)/shard_map/all_to_all | solution.py:178
  170.4 3.3 %multiply_reduce_fusion.7 = (f32[]{:T(128)}, f32[128]{0:T(128)S(1)}, f32[128]{0:T(128)}) fusion(f32[32,128]{1,0:T(8,128)S(1)} %reshape.268, s32[]{:T(128)S(6)} %select_n.47, s32[1,128]{1,0:T(1,128)S(1)} %copy-done.10, f32[128]{0:T(128)S(1)} %get-tuple-element.47, f32[4096,1]{0,1:T(1,128)S(1)} %bitcast.153, bf16[1,128,4096]{2,1,0:T(8,128)(2,1)} %param.12), kind=kOutput, calls=%fused_computation.129 | convolution fusion | flops 6292223 | bytes 1067528 | tf_op jit(solution)/shard_map/dot_general | solution.py:157
  174.6 2.5 %all-to-all-start.5 = ((f32[32,1,48]{2,1,0:T(1,128)}), f32[32,1,48]{2,1,0:T(1,128)S(1)}, u32[]{:S(2)}, u32[]{:S(2)}) async-start(f32[32,1,48]{2,1,0:T(1,128)} %bitcast.42), calls=%async_computation.5 | async-start | bytes 32768 | tf_op jit(solution)/shard_map/all_to_all | solution.py:195
  177.2 2.1 fusion.40
  179.3 1.8 fusion.31
  181.8 2.4 %all-to-all-done.5 = f32[32,1,48]{2,1,0:T(1,128)S(1)} async-done(((f32[32,1,48]{2,1,0:T(1,128)}), f32[32,1,48]{2,1,0:T(1,128)S(1)}, u32[]{:S(2)}, u32[]{:S(2)}) %all-to-all-start.5) | async-done | bytes 6176 | tf_op jit(solution)/shard_map/all_to_all | solution.py:195
  184.5 1.6 multiply_reduce_fusion
  186.1 3.2 %fusion.2 = f32[1,4096]{1,0:T(1,128)S(1)} fusion(f32[384,1]{0,1:T(1,128)S(1)} %reshape.278, bf16[1,384,4096]{2,1,0:T(8,128)(2,1)} %param.18), kind=kOutput, calls=%fused_computation.10 | convolution fusion | flops 18874368 | bytes 3163648 | tf_op jit(solution)/shard_map/dot_general | solution.py:212
  190.1 3.7 %all-to-all-start.6 = ((f32[32,10,128]{2,1,0:T(8,128)}), f32[32,10,128]{2,1,0:T(8,128)S(1)}, u32[]{:S(2)}, u32[]{:S(2)}) async-start(f32[32,10,128]{2,1,0:T(8,128)} %maximum_bitcast_fusion), calls=%async_computation.6 | async-start | bytes 524288 | tf_op jit(solution)/shard_map/all_to_all | solution.py:219
  193.8 10.3 %fusion = bf16[1,384,4096]{2,1,0:T(8,128)(2,1)} fusion(bf16[512,4096]{1,0:T(8,128)(2,1)} %bitcast.138, bf16[512,4096]{1,0:T(8,128)(2,1)} %bitcast.134, bf16[512,4096]{1,0:T(8,128)(2,1)} %bitcast.129, f32[512,384]{1,0:T(8,128)} %get-tuple-element.57, f32[512,384]{1,0:T(8,128)} %get-tuple-element.56, f32[512,384]{1,0:T(8,128)} %get-tuple-element.55, ...), kind=kOutput, calls=%fused_computation.5 | convolution fusion | flops 4873519104 | bytes 18094080 | tf_op jit(solution)/shard_map/dot_general | solution.py:223
  204.1 8.7 %fusion.1 = bf16[1,384,4096]{2,1,0:T(8,128)(2,1)} fusion(bf16[512,4096]{1,0:T(8,128)(2,1)} %bitcast.139, bf16[512,4096]{1,0:T(8,128)(2,1)S(1)} %bitcast.135, bf16[512,4096]{1,0:T(8,128)(2,1)S(1)} %bitcast.131, f32[512,384]{1,0:T(8,128)} %get-tuple-element.60, f32[512,384]{1,0:T(8,128)} %get-tuple-element.59, f32[512,384]{1,0:T(8,128)S(1)} %copy-done.13, ...), kind=kOutput, calls=%fused_computation.6 | convolution fusion | flops 4873519104 | bytes 18094080 | tf_op jit(solution)/shard_map/dot_general | solution.py:223
  213.6 5.6 %all-to-all-start.7 = ((f32[32,10,128]{2,1,0:T(8,128)}), f32[32,10,128]{2,1,0:T(8,128)S(1)}, u32[]{:S(2)}, u32[]{:S(2)}) async-start(f32[32,10,128]{2,1,0:T(8,128)} %broadcast_in_dim.190), calls=%async_computation.7 | async-start | bytes 524288 | tf_op jit(solution)/shard_map/all_to_all | solution.py:45
  219.1 2.3 multiply_convert_fusion
  221.4 8.3 %all-to-all-done.7 = f32[32,10,128]{2,1,0:T(8,128)S(1)} async-done(((f32[32,10,128]{2,1,0:T(8,128)}), f32[32,10,128]{2,1,0:T(8,128)S(1)}, u32[]{:S(2)}, u32[]{:S(2)}) %all-to-all-start.7) | async-done | bytes 163872 | tf_op jit(solution)/shard_map/all_to_all | solution.py:45
  (130 shorter events, 16.2 us)
Async XLA Ops:
  0.6 109.2 %copy-start = (bf16[1,384,4096]{2,1,0:T(8,128)(2,1)S(1)}, bf16[1,384,4096]{2,1,0:T(8,128)(2,1)}, u32[]{:S(2)}) copy-start(bf16[1,384,4096]{2,1,0:T(8,128)(2,1)} %param.17) | copy-start | bytes 9437188
  4.3 14.6 %all-to-all-start.4 = ((f32[32,4,128]{2,1,0:T(4,128)}), f32[32,4,128]{2,1,0:T(4,128)S(1)}, u32[]{:S(2)}, u32[]{:S(2)}) async-start(f32[32,4,128]{2,1,0:T(4,128)} %broadcast_in_dim.180), calls=%async_computation.4 | async-start | bytes 131072 | tf_op jit(solution)/shard_map/all_to_all | solution.py:45
  16.9 7.9 %copy-start.9 = (f32[4096]{0:T(1024)S(1)}, f32[4096]{0:T(1024)}, u32[]{:S(2)}) copy-start(f32[4096]{0:T(1024)} %param.13) | copy-start | bytes 49156
  18.7 8.4 %copy-start.8 = (f32[4096]{0:T(1024)S(1)}, f32[4096]{0:T(1024)}, u32[]{:S(2)}) copy-start(f32[4096]{0:T(1024)} %param.15) | copy-start | bytes 49156
  18.9 31.9 %all-to-all-start = ((bf16[8,16,4096]{2,1,0:T(8,128)(2,1)}), bf16[8,16,4096]{2,1,0:T(8,128)(2,1)}, u32[]{:S(2)}, u32[]{:S(2)}) async-start(bf16[8,16,4096]{2,1,0:T(8,128)(2,1)} %get-tuple-element.53), calls=%async_computation | async-start | bytes 2097152 | tf_op jit(solution)/shard_map/all_to_all | solution.py:63
  24.7 6.9 %copy-start.1 = (bf16[1,128,4096]{2,1,0:T(8,128)(2,1)S(1)}, bf16[1,128,4096]{2,1,0:T(8,128)(2,1)}, u32[]{:S(2)}) copy-start(bf16[1,128,4096]{2,1,0:T(8,128)(2,1)} %param.12) | copy-start | bytes 3145732
  50.8 29.9 %all-to-all-start.1 = ((bf16[8,16,4096]{2,1,0:T(8,128)(2,1)}), bf16[8,16,4096]{2,1,0:T(8,128)(2,1)}, u32[]{:S(2)}, u32[]{:S(2)}) async-start(bf16[8,16,4096]{2,1,0:T(8,128)(2,1)} %get-tuple-element.52), calls=%async_computation.1 | async-start | bytes 2097152 | tf_op jit(solution)/shard_map/all_to_all | solution.py:63
  58.5 25.6 %collective-permute-start = (bf16[8,16,4096]{2,1,0:T(8,128)(2,1)}, bf16[8,16,4096]{2,1,0:T(8,128)(2,1)}, u32[]{:S(2)}, u32[]{:S(2)}) collective-permute-start(bf16[8,16,4096]{2,1,0:T(8,128)(2,1)} %all-to-all-done), channel_id=1, source_target_pairs={{0,16},{8,24},{16,0},{24,8},{1,17},{9,25},{17,1},{25,9},{2,18},{10... | collective-permute-start | bytes 3145736 | tf_op jit(solution)/shard_map/ppermute | solution.py:51
  80.7 24.7 %collective-permute-start.4 = (bf16[8,16,4096]{2,1,0:T(8,128)(2,1)}, bf16[8,16,4096]{2,1,0:T(8,128)(2,1)}, u32[]{:S(2)}, u32[]{:S(2)}) collective-permute-start(bf16[8,16,4096]{2,1,0:T(8,128)(2,1)} %all-to-all-done.1), channel_id=1, source_target_pairs={{0,16},{8,24},{16,0},{24,8},{1,17},{9,25},{17,1},{25,9},{2,18},{10... | collective-permute-start | bytes 3145736 | tf_op jit(solution)/shard_map/ppermute | solution.py:51
  84.0 21.4 %collective-permute-start.1 = (bf16[8,16,4096]{2,1,0:T(8,128)(2,1)}, bf16[8,16,4096]{2,1,0:T(8,128)(2,1)}, u32[]{:S(2)}, u32[]{:S(2)}) collective-permute-start(bf16[8,16,4096]{2,1,0:T(8,128)(2,1)} %all-to-all-done), channel_id=1, source_target_pairs={{0,8},{8,0},{16,24},{24,16},{1,9},{9,1},{17,25},{25,17},{2,10},{10... | collective-permute-start | bytes 3145736 | tf_op jit(solution)/shard_map/ppermute | solution.py:51
  84.0 21.4 %collective-permute-start.2 = (bf16[8,16,4096]{2,1,0:T(8,128)(2,1)}, bf16[8,16,4096]{2,1,0:T(8,128)(2,1)}, u32[]{:S(2)}, u32[]{:S(2)}) collective-permute-start(bf16[8,16,4096]{2,1,0:T(8,128)(2,1)} %collective-permute-done), channel_id=1, source_target_pairs={{0,8},{8,0},{16,24},{24,16},{1,9},{9,1},{17,25},{25,17},{2,10},{10... | collective-permute-start | bytes 3145736 | tf_op jit(solution)/shard_map/ppermute | solution.py:51
  84.8 32.3 %all-to-all-start.2 = ((bf16[8,16,4096]{2,1,0:T(8,128)(2,1)}), bf16[8,16,4096]{2,1,0:T(8,128)(2,1)}, u32[]{:S(2)}, u32[]{:S(2)}) async-start(bf16[8,16,4096]{2,1,0:T(8,128)(2,1)} %get-tuple-element.12), calls=%async_computation.2 | async-start | bytes 2097152 | tf_op jit(solution)/shard_map/all_to_all | solution.py:63
  94.4 24.2 %collective-permute-start.3 = (bf16[8,16,4096]{2,1,0:T(8,128)(2,1)}, bf16[8,16,4096]{2,1,0:T(8,128)(2,1)}, u32[]{:S(2)}, u32[]{:S(2)}) collective-permute-start(bf16[8,16,4096]{2,1,0:T(8,128)(2,1)} %all-to-all-done.1), channel_id=1, source_target_pairs={{0,8},{8,0},{16,24},{24,16},{1,9},{9,1},{17,25},{25,17},{2,10},{10... | collective-permute-start | bytes 3145736 | tf_op jit(solution)/shard_map/ppermute | solution.py:51
  105.5 13.2 %collective-permute-start.5 = (bf16[8,16,4096]{2,1,0:T(8,128)(2,1)}, bf16[8,16,4096]{2,1,0:T(8,128)(2,1)}, u32[]{:S(2)}, u32[]{:S(2)}) collective-permute-start(bf16[8,16,4096]{2,1,0:T(8,128)(2,1)} %collective-permute-done.4), channel_id=1, source_target_pairs={{0,8},{8,0},{16,24},{24,16},{1,9},{9,1},{17,25},{25,17},{2,10},{10... | collective-permute-start | bytes 3145736 | tf_op jit(solution)/shard_map/ppermute | solution.py:51
  107.9 1.9 copy-start.2
  117.1 24.2 %collective-permute-start.7 = (bf16[8,16,4096]{2,1,0:T(8,128)(2,1)}, bf16[8,16,4096]{2,1,0:T(8,128)(2,1)S(1)}, u32[]{:S(2)}, u32[]{:S(2)}) collective-permute-start(bf16[8,16,4096]{2,1,0:T(8,128)(2,1)} %all-to-all-done.2), channel_id=1, source_target_pairs={{0,16},{8,24},{16,0},{24,8},{1,17},{9,25},{17,1},{25,9},{2,18},{10... | collective-permute-start | bytes 3145736 | tf_op jit(solution)/shard_map/ppermute | solution.py:51
  118.6 3.4 %copy-start.3 = (bf16[4,8,16,4096]{3,2,1,0:T(8,128)(2,1)S(1)}, bf16[4,8,16,4096]{3,2,1,0:T(8,128)(2,1)}, u32[]{:S(2)}) copy-start(bf16[4,8,16,4096]{3,2,1,0:T(8,128)(2,1)} %copy-done.2) | copy-start | bytes 12582916
  118.6 4.4 %copy-start.11 = (bf16[1,384,4096]{2,1,0:T(8,128)(2,1)S(1)}, bf16[1,384,4096]{2,1,0:T(8,128)(2,1)}, u32[]{:S(2)}) copy-start(bf16[1,384,4096]{2,1,0:T(8,128)(2,1)} %param.16) | copy-start | bytes 9437188
  123.1 20.6 %copy-start.5 = (bf16[4,8,16,4096]{3,2,1,0:T(8,128)(2,1)}, bf16[4,8,16,4096]{3,2,1,0:T(8,128)(2,1)S(1)}, u32[]{:S(2)}) copy-start(bf16[4,8,16,4096]{3,2,1,0:T(8,128)(2,1)S(1)} %pad_maximum_fusion.4) | copy-start | bytes 12582916
  125.4 20.6 %collective-permute-start.6 = (bf16[8,16,4096]{2,1,0:T(8,128)(2,1)}, bf16[8,16,4096]{2,1,0:T(8,128)(2,1)S(1)}, u32[]{:S(2)}, u32[]{:S(2)}) collective-permute-start(bf16[8,16,4096]{2,1,0:T(8,128)(2,1)} %all-to-all-done.2), channel_id=1, source_target_pairs={{0,8},{8,0},{16,24},{24,16},{1,9},{9,1},{17,25},{25,17},{2,10},{10... | collective-permute-start | bytes 3145736 | tf_op jit(solution)/shard_map/ppermute | solution.py:51
  141.3 4.8 %collective-permute-start.8 = (bf16[8,16,4096]{2,1,0:T(8,128)(2,1)S(1)}, bf16[8,16,4096]{2,1,0:T(8,128)(2,1)S(1)}, u32[]{:S(2)}, u32[]{:S(2)}) collective-permute-start(bf16[8,16,4096]{2,1,0:T(8,128)(2,1)S(1)} %collective-permute-done.7), channel_id=1, source_target_pairs={{0,8},{8,0},{16,24},{24,16},{1,9},{9,1},{17,25},{25,17},{2,10},{10... | collective-permute-start | bytes 3145736 | tf_op jit(solution)/shard_map/ppermute | solution.py:51
  147.9 2.4 %copy-start.7 = (bf16[4,8,16,4096]{3,2,1,0:T(8,128)(2,1)}, bf16[4,8,16,4096]{3,2,1,0:T(8,128)(2,1)S(1)}, u32[]{:S(2)}) copy-start(bf16[4,8,16,4096]{3,2,1,0:T(8,128)(2,1)S(1)} %pad_maximum_fusion.5) | copy-start | bytes 12582916
  147.9 2.4 %copy-start.12 = (f32[512,384]{1,0:T(8,128)S(1)}, f32[512,384]{1,0:T(8,128)}, u32[]{:S(2)}) copy-start(f32[512,384]{1,0:T(8,128)} %fusion.10) | copy-start | bytes 2359300
  150.3 20.1 %copy-start.10 = (s32[1,128]{1,0:T(1,128)S(1)}, s32[1,128]{1,0:T(1,128)}, u32[]{:S(2)}) copy-start(s32[1,128]{1,0:T(1,128)} %param.21) | copy-start | bytes 1540
  156.9 11.9 %all-to-all-start.3 = ((f32[32,1,48]{2,1,0:T(1,128)}), f32[32,1,48]{2,1,0:T(1,128)S(1)}, u32[]{:S(2)}, u32[]{:S(2)}) async-start(f32[32,1,48]{2,1,0:T(1,128)} %bitcast.25), calls=%async_computation.3 | async-start | bytes 32768 | tf_op jit(solution)/shard_map/all_to_all | solution.py:178
  174.6 9.6 %all-to-all-start.5 = ((f32[32,1,48]{2,1,0:T(1,128)}), f32[32,1,48]{2,1,0:T(1,128)S(1)}, u32[]{:S(2)}, u32[]{:S(2)}) async-start(f32[32,1,48]{2,1,0:T(1,128)} %bitcast.42), calls=%async_computation.5 | async-start | bytes 32768 | tf_op jit(solution)/shard_map/all_to_all | solution.py:195
  190.1 22.7 %all-to-all-start.6 = ((f32[32,10,128]{2,1,0:T(8,128)}), f32[32,10,128]{2,1,0:T(8,128)S(1)}, u32[]{:S(2)}, u32[]{:S(2)}) async-start(f32[32,10,128]{2,1,0:T(8,128)} %maximum_bitcast_fusion), calls=%async_computation.6 | async-start | bytes 524288 | tf_op jit(solution)/shard_map/all_to_all | solution.py:219
  193.8 10.3 %copy-start.4 = (bf16[4,8,16,4096]{3,2,1,0:T(8,128)(2,1)S(1)}, bf16[4,8,16,4096]{3,2,1,0:T(8,128)(2,1)}, u32[]{:S(2)}) copy-start(bf16[4,8,16,4096]{3,2,1,0:T(8,128)(2,1)} %copy-done.2) | copy-start | bytes 12582916
  193.8 10.3 %copy-start.6 = (bf16[4,8,16,4096]{3,2,1,0:T(8,128)(2,1)S(1)}, bf16[4,8,16,4096]{3,2,1,0:T(8,128)(2,1)}, u32[]{:S(2)}) copy-start(bf16[4,8,16,4096]{3,2,1,0:T(8,128)(2,1)} %copy-done.5) | copy-start | bytes 12582916
  193.8 10.3 %copy-start.13 = (f32[512,384]{1,0:T(8,128)S(1)}, f32[512,384]{1,0:T(8,128)}, u32[]{:S(2)}) copy-start(f32[512,384]{1,0:T(8,128)} %get-tuple-element.58) | copy-start | bytes 2359300
  213.6 16.2 %all-to-all-start.7 = ((f32[32,10,128]{2,1,0:T(8,128)}), f32[32,10,128]{2,1,0:T(8,128)S(1)}, u32[]{:S(2)}, u32[]{:S(2)}) async-start(f32[32,10,128]{2,1,0:T(8,128)} %broadcast_in_dim.190), calls=%async_computation.7 | async-start | bytes 524288 | tf_op jit(solution)/shard_map/all_to_all | solution.py:45
